TPU v7x, 256 devices: a whole 4x4x8 slice. The times are simulated.
256 devices in a mesh: grp: 16 (over x, y_hi, core), blk: 16 (over y_lo, z).
Axes of the slice: x: 4, y: 4 (y_hi: 2, y_lo: 2; y = y_hi * 2 + y_lo), z: 8, core: 2. Of those that a mesh axis runs over, the one named last changes fastest.
Arguments:
- embeddings: bfloat16 [65536, 512], P(('grp', 'blk'))
- cluster: int32 [65536], P(('grp', 'blk')), may hold values from 0 to 47, as said below
- order: int32 [65536], P(('grp', 'blk')), may hold values from 0 to 65535, each once
Outputs:
- nearest: float32 [65536], P(('grp', 'blk'))
Inputs may be any that keep to these rules, and one draw needn't show every extreme that they name: Cluster c belongs to cluster set c // 3. The 256 rows of one device hold at most 48 rows of any one cluster set, and in every draw exactly 48 rows of some set.
All inputs are finite; a program needn't handle non-finite values.
Results may differ from a plain program's by a relative error of at most 0.00057.
Values may be sent and summed in bfloat16 or wider, within the bound.
A program may use at most 64 MiB of HBM per device.

v0:
```python
import jax
import jax.numpy as jnp
from jax import lax
from jax.sharding import PartitionSpec as P


def from_behind(x, axis, by):
    size = lax.axis_size(axis)
    return lax.ppermute(x, axis, [(i, (i + by) % size) for i in range(size)])


def fold_block(best, local, block):
    local_unit, local_cl, local_ord = local
    block_unit, block_cl, block_ord = block
    score = lax.dot_general(
        local_unit, block_unit, (((1,), (1,)), ((), ())), preferred_element_type=jnp.float32
    )
    keep = (
        (local_cl[:, None] == block_cl[None, :])
        & (local_cl[:, None] >= 0)
        & (block_ord[None, :] < local_ord[:, None])
    )
    return jnp.maximum(best, jnp.max(jnp.where(keep, score, jnp.float32(-1.0)), axis=1))


def body(embeddings, cluster, order):
    rows, width = embeddings.shape
    groups = lax.axis_size("grp")
    owners = lax.axis_size("blk")
    capacity = 3 * rows // groups
    values = embeddings.astype(jnp.float32)
    unit = (values * lax.rsqrt(jnp.sum(values * values, axis=1, keepdims=True) + 1e-06)).astype(
        jnp.bfloat16
    )
    target = cluster // 3
    onehot = (target[:, None] == jnp.arange(groups, dtype=jnp.int32)[None, :]).astype(jnp.int32)
    slot = jnp.sum((jnp.cumsum(onehot, axis=0) - 1) * onehot, axis=1)
    send_unit = jnp.zeros((groups, capacity, width), jnp.bfloat16).at[target, slot].set(unit)
    send_cl = jnp.full((groups, capacity), -1, jnp.int32).at[target, slot].set(cluster)
    send_ord = jnp.zeros((groups, capacity), jnp.int32).at[target, slot].set(order)
    got_unit, got_cl, got_ord = (
        lax.all_to_all(send_unit, "grp", split_axis=0, concat_axis=0, tiled=True),
        lax.all_to_all(send_cl, "grp", split_axis=0, concat_axis=0, tiled=True),
        lax.all_to_all(send_ord, "grp", split_axis=0, concat_axis=0, tiled=True),
    )
    slots = groups * capacity
    local = (got_unit.reshape(slots, width), got_cl.reshape(slots), got_ord.reshape(slots))
    empty = jnp.full((slots,), -1.0, jnp.float32)
    best = fold_block(empty, local, local)

    def step_one(turn, carry):
        best_now, moving = carry
        moving = from_behind((moving[0], moving[1], moving[2]), "blk", 1)
        return (fold_block(best_now, local, moving), moving)

    best, moving = lax.fori_loop(0, owners - 1, step_one, (best, local))
    back = lax.all_to_all(
        best.reshape(groups, capacity), "grp", split_axis=0, concat_axis=0, tiled=True
    )
    return back[target, slot]


def solution(mesh):
    return jax.shard_map(
        body,
        mesh=mesh,
        in_specs=(P(("grp", "blk"), None), P(("grp", "blk")), P(("grp", "blk"))),
        out_specs=P(("grp", "blk")),
        check_vma=False,
    )
```

profile of v0, /device:TPU:1, one launch (start us, length us, event | category | flops | bytes accessed | tf_op | source)
XLA Modules:
  0.0 459.2 jit_solution(6093896044848572583)
XLA Ops:
  0.0 0.7 compare_select_fusion.1
  2.2 35.4 %scatter_fusion.1 = s32[16,48]{1,0:T(8,128)} fusion(s32[16,48]{1,0:T(8,128)} %broadcast_in_dim.36, s32[256]{0:T(256)S(1)} %bitcast.40, s32[256]{0:T(256)} %param.7), kind=kCustom, calls=%fused_computation.2 | custom fusion | bytes 5120 | tf_op jit(solution)/shard_map/scatter | solution.py:40
  37.7 8.4 %all-to-all-start.1 = ((s32[16,1,48]{2,1,0:T(1,128)}), s32[16,1,48]{2,1,0:T(1,128)S(1)}, u32[]{:S(2)}, u32[]{:S(2)}) async-start(s32[16,1,48]{2,1,0:T(1,128)} %bitcast.8), calls=%async_computation.1 | async-start | bytes 16384 | tf_op jit(solution)/shard_map/all_to_all | solution.py:44
  46.8 35.3 %scatter_fusion = s32[16,48]{1,0:T(8,128)} fusion(s32[16,48]{1,0:T(8,128)} %broadcast_in_dim.19, s32[256]{0:T(256)S(1)} %bitcast.41, s32[256]{0:T(256)S(1)} %copy-done.3), kind=kCustom, calls=%fused_computation.1 | custom fusion | bytes 5120 | tf_op jit(solution)/shard_map/scatter | solution.py:39
  82.1 7.3 %all-to-all-start = ((s32[16,1,48]{2,1,0:T(1,128)}), s32[16,1,48]{2,1,0:T(1,128)S(1)}, u32[]{:S(2)}, u32[]{:S(2)}) async-start(s32[16,1,48]{2,1,0:T(1,128)} %bitcast.6), calls=%async_computation | async-start | bytes 16384 | tf_op jit(solution)/shard_map/all_to_all | solution.py:43
  89.6 1.0 broadcast_in_dim.37
  90.5 32.6 %scatter_fusion.2 = bf16[16,48,512]{2,1,0:T(8,128)(2,1)} fusion(bf16[16,48,512]{2,1,0:T(8,128)(2,1)} %broadcast_in_dim.37, s32[256]{0:T(256)S(1)} %bitcast.42, bf16[256,512]{1,0:T(8,128)(2,1)S(1)} %fusion.1), kind=kCustom, calls=%fused_computation.3 | custom fusion | bytes 788480 | tf_op jit(solution)/shard_map/scatter | solution.py:38
  123.2 7.1 %all-to-all-start.2 = ((bf16[16,48,512]{2,1,0:T(8,128)(2,1)}), bf16[16,48,512]{2,1,0:T(8,128)(2,1)S(1)}, u32[]{:S(2)}, u32[]{:S(2)}) async-start(bf16[16,48,512]{2,1,0:T(8,128)(2,1)} %scatter_fusion.2), calls=%async_computation.2 | async-start | bytes 1572864 | tf_op jit(solution)/shard_map/all_to_all | solution.py:42
  131.6 0.7 reduce.9
  132.5 12.0 %all-to-all-done.2 = bf16[16,48,512]{2,1,0:T(8,128)(2,1)S(1)} async-done(((bf16[16,48,512]{2,1,0:T(8,128)(2,1)}), bf16[16,48,512]{2,1,0:T(8,128)(2,1)S(1)}, u32[]{:S(2)}, u32[]{:S(2)}) %all-to-all-start.2) | async-done | bytes 786464 | tf_op jit(solution)/shard_map/all_to_all | solution.py:42
  144.5 1.1 select_reduce_fusion.1
  145.6 285.8 %while.17 = (s32[]{:T(128)}, f32[768]{0:T(1024)S(1)}, bf16[768,512]{1,0:T(8,128)(2,1)S(1)}, s32[768]{0:T(1024)S(1)}, s32[768]{0:T(1024)S(1)}, /*index=5*/s32[16,...) while((s32[]{:T(128)}, f32[768]{0:T(1024)S(1)}, ...), condition=%wide.wide.region_10.11_spmd, body=%wide.wide.region_8.10_spmd.sunk | while | flops 607519488 | bytes 6357733 | solution.py:56
  145.6 1.9 collective-permute-start.2
  147.5 1.4 collective-permute-start
  148.9 2.3 collective-permute-start.1
  151.2 17.4 %collective-permute-done.1 = s32[768]{0:T(1024)S(1)} collective-permute-done((s32[768]{0:T(1024)S(1)}, s32[768]{0:T(1024)S(1)}, u32[]{:S(2)}, u32[]{:S(2)}) %collective-permute-start.1) | collective-permute-done | bytes 3104 | tf_op jit(solution)/shard_map/while/body/eval_jaxpr/ppermute | solution.py:9
  168.6 1.0 select_reduce_fusion.4
  169.9 1.2 collective-permute-start.1
  171.1 18.3 %collective-permute-done.1 = s32[768]{0:T(1024)S(1)} collective-permute-done((s32[768]{0:T(1024)S(1)}, s32[768]{0:T(1024)S(1)}, u32[]{:S(2)}, u32[]{:S(2)}) %collective-permute-start.1) | collective-permute-done | bytes 3104 | tf_op jit(solution)/shard_map/while/body/eval_jaxpr/ppermute | solution.py:9
  189.4 1.0 select_reduce_fusion.4
  190.8 18.4 %collective-permute-done.1 = s32[768]{0:T(1024)S(1)} collective-permute-done((s32[768]{0:T(1024)S(1)}, s32[768]{0:T(1024)S(1)}, u32[]{:S(2)}, u32[]{:S(2)}) %collective-permute-start.1) | collective-permute-done | bytes 3104 | tf_op jit(solution)/shard_map/while/body/eval_jaxpr/ppermute | solution.py:9
  209.3 1.0 select_reduce_fusion.4
  210.7 17.5 %collective-permute-done.1 = s32[768]{0:T(1024)S(1)} collective-permute-done((s32[768]{0:T(1024)S(1)}, s32[768]{0:T(1024)S(1)}, u32[]{:S(2)}, u32[]{:S(2)}) %collective-permute-start.1) | collective-permute-done | bytes 3104 | tf_op jit(solution)/shard_map/while/body/eval_jaxpr/ppermute | solution.py:9
  228.2 1.0 select_reduce_fusion.4
  229.6 16.6 %collective-permute-done.1 = s32[768]{0:T(1024)S(1)} collective-permute-done((s32[768]{0:T(1024)S(1)}, s32[768]{0:T(1024)S(1)}, u32[]{:S(2)}, u32[]{:S(2)}) %collective-permute-start.1) | collective-permute-done | bytes 3104 | tf_op jit(solution)/shard_map/while/body/eval_jaxpr/ppermute | solution.py:9
  246.2 1.1 select_reduce_fusion.4
  247.7 15.7 %collective-permute-done.1 = s32[768]{0:T(1024)S(1)} collective-permute-done((s32[768]{0:T(1024)S(1)}, s32[768]{0:T(1024)S(1)}, u32[]{:S(2)}, u32[]{:S(2)}) %collective-permute-start.1) | collective-permute-done | bytes 3104 | tf_op jit(solution)/shard_map/while/body/eval_jaxpr/ppermute | solution.py:9
  263.4 1.0 select_reduce_fusion.4
  264.8 14.7 %collective-permute-done.1 = s32[768]{0:T(1024)S(1)} collective-permute-done((s32[768]{0:T(1024)S(1)}, s32[768]{0:T(1024)S(1)}, u32[]{:S(2)}, u32[]{:S(2)}) %collective-permute-start.1) | collective-permute-done | bytes 3104 | tf_op jit(solution)/shard_map/while/body/eval_jaxpr/ppermute | solution.py:9
  279.5 1.0 select_reduce_fusion.4
  281.0 14.7 %collective-permute-done.1 = s32[768]{0:T(1024)S(1)} collective-permute-done((s32[768]{0:T(1024)S(1)}, s32[768]{0:T(1024)S(1)}, u32[]{:S(2)}, u32[]{:S(2)}) %collective-permute-start.1) | collective-permute-done | bytes 3104 | tf_op jit(solution)/shard_map/while/body/eval_jaxpr/ppermute | solution.py:9
  295.7 1.0 select_reduce_fusion.4
  297.1 14.5 %collective-permute-done.1 = s32[768]{0:T(1024)S(1)} collective-permute-done((s32[768]{0:T(1024)S(1)}, s32[768]{0:T(1024)S(1)}, u32[]{:S(2)}, u32[]{:S(2)}) %collective-permute-start.1) | collective-permute-done | bytes 3104 | tf_op jit(solution)/shard_map/while/body/eval_jaxpr/ppermute | solution.py:9
  311.7 1.0 select_reduce_fusion.4
  313.1 15.6 %collective-permute-done.1 = s32[768]{0:T(1024)S(1)} collective-permute-done((s32[768]{0:T(1024)S(1)}, s32[768]{0:T(1024)S(1)}, u32[]{:S(2)}, u32[]{:S(2)}) %collective-permute-start.1) | collective-permute-done | bytes 3104 | tf_op jit(solution)/shard_map/while/body/eval_jaxpr/ppermute | solution.py:9
  328.7 1.0 select_reduce_fusion.4
  330.2 16.7 %collective-permute-done.1 = s32[768]{0:T(1024)S(1)} collective-permute-done((s32[768]{0:T(1024)S(1)}, s32[768]{0:T(1024)S(1)}, u32[]{:S(2)}, u32[]{:S(2)}) %collective-permute-start.1) | collective-permute-done | bytes 3104 | tf_op jit(solution)/shard_map/while/body/eval_jaxpr/ppermute | solution.py:9
  346.9 1.0 select_reduce_fusion.4
  348.3 17.8 %collective-permute-done.1 = s32[768]{0:T(1024)S(1)} collective-permute-done((s32[768]{0:T(1024)S(1)}, s32[768]{0:T(1024)S(1)}, u32[]{:S(2)}, u32[]{:S(2)}) %collective-permute-start.1) | collective-permute-done | bytes 3104 | tf_op jit(solution)/shard_map/while/body/eval_jaxpr/ppermute | solution.py:9
  366.1 1.0 select_reduce_fusion.4
  367.5 18.9 %collective-permute-done.1 = s32[768]{0:T(1024)S(1)} collective-permute-done((s32[768]{0:T(1024)S(1)}, s32[768]{0:T(1024)S(1)}, u32[]{:S(2)}, u32[]{:S(2)}) %collective-permute-start.1) | collective-permute-done | bytes 3104 | tf_op jit(solution)/shard_map/while/body/eval_jaxpr/ppermute | solution.py:9
  386.4 1.1 select_reduce_fusion.4
  387.8 19.9 %collective-permute-done.1 = s32[768]{0:T(1024)S(1)} collective-permute-done((s32[768]{0:T(1024)S(1)}, s32[768]{0:T(1024)S(1)}, u32[]{:S(2)}, u32[]{:S(2)}) %collective-permute-start.1) | collective-permute-done | bytes 3104 | tf_op jit(solution)/shard_map/while/body/eval_jaxpr/ppermute | solution.py:9
  407.8 1.0 select_reduce_fusion.4
  409.2 21.0 %collective-permute-done.1 = s32[768]{0:T(1024)S(1)} collective-permute-done((s32[768]{0:T(1024)S(1)}, s32[768]{0:T(1024)S(1)}, u32[]{:S(2)}, u32[]{:S(2)}) %collective-permute-start.1) | collective-permute-done | bytes 3104 | tf_op jit(solution)/shard_map/while/body/eval_jaxpr/ppermute | solution.py:9
  430.3 1.0 select_reduce_fusion.4
  431.5 25.2 %all_to_all.41 = f32[16,1,48]{2,1,0:T(1,128)S(1)} all-to-all(f32[16,1,48]{2,1,0:T(1,128)S(1)} %all_to_all.34), channel_id=1, replica_groups=mesh['grp'=16,'blk'=16] {'grp'}, dimensions={0} | all-to-all | bytes 6144 | tf_op jit(solution)/shard_map/all_to_all | solution.py:57
  456.7 2.5 gather_fusion
  (178 shorter events, 8.5 us)
Async XLA Ops:
  37.7 44.4 %all-to-all-start.1 = ((s32[16,1,48]{2,1,0:T(1,128)}), s32[16,1,48]{2,1,0:T(1,128)S(1)}, u32[]{:S(2)}, u32[]{:S(2)}) async-start(s32[16,1,48]{2,1,0:T(1,128)} %bitcast.8), calls=%async_computation.1 | async-start | bytes 16384 | tf_op jit(solution)/shard_map/all_to_all | solution.py:44
  82.1 41.0 %all-to-all-start = ((s32[16,1,48]{2,1,0:T(1,128)}), s32[16,1,48]{2,1,0:T(1,128)S(1)}, u32[]{:S(2)}, u32[]{:S(2)}) async-start(s32[16,1,48]{2,1,0:T(1,128)} %bitcast.6), calls=%async_computation | async-start | bytes 16384 | tf_op jit(solution)/shard_map/all_to_all | solution.py:43
  123.2 21.3 %all-to-all-start.2 = ((bf16[16,48,512]{2,1,0:T(8,128)(2,1)}), bf16[16,48,512]{2,1,0:T(8,128)(2,1)S(1)}, u32[]{:S(2)}, u32[]{:S(2)}) async-start(bf16[16,48,512]{2,1,0:T(8,128)(2,1)} %scatter_fusion.2), calls=%async_computation.2 | async-start | bytes 1572864 | tf_op jit(solution)/shard_map/all_to_all | solution.py:42
  145.6 23.0 %collective-permute-start.2 = (bf16[768,512]{1,0:T(8,128)(2,1)S(1)}, bf16[768,512]{1,0:T(8,128)(2,1)S(1)}, u32[]{:S(2)}, u32[]{:S(2)}) collective-permute-start(bf16[768,512]{1,0:T(8,128)(2,1)S(1)} %get-tuple-element.173), channel_id=1, source_target_pairs={{0,1},{1,2},{2,3},{3,4},{4,5},{5,6},{6,7},{7,8},{8,9},{9,10},{10,1... | collective-permute-start | bytes 2359304 | tf_op jit(solution)/shard_map/while/body/eval_jaxpr/ppermute | solution.py:9
  147.5 21.1 %collective-permute-start = (s32[768]{0:T(1024)S(1)}, s32[768]{0:T(1024)S(1)}, u32[]{:S(2)}, u32[]{:S(2)}) collective-permute-start(s32[768]{0:T(1024)S(1)} %get-tuple-element.175), channel_id=1, source_target_pairs={{0,1},{1,2},{2,3},{3,4},{4,5},{5,6},{6,7},{7,8},{8,9},{9,10},{10,1... | collective-permute-start | bytes 9224 | tf_op jit(solution)/shard_map/while/body/eval_jaxpr/ppermute | solution.py:9
  148.9 19.7 %collective-permute-start.1 = (s32[768]{0:T(1024)S(1)}, s32[768]{0:T(1024)S(1)}, u32[]{:S(2)}, u32[]{:S(2)}) collective-permute-start(s32[768]{0:T(1024)S(1)} %get-tuple-element.174), channel_id=1, source_target_pairs={{0,1},{1,2},{2,3},{3,4},{4,5},{5,6},{6,7},{7,8},{8,9},{9,10},{10,1... | collective-permute-start | bytes 9224 | tf_op jit(solution)/shard_map/while/body/eval_jaxpr/ppermute | solution.py:9
  169.8 19.7 %collective-permute-start.2 = (bf16[768,512]{1,0:T(8,128)(2,1)S(1)}, bf16[768,512]{1,0:T(8,128)(2,1)S(1)}, u32[]{:S(2)}, u32[]{:S(2)}) collective-permute-start(bf16[768,512]{1,0:T(8,128)(2,1)S(1)} %get-tuple-element.173), channel_id=1, source_target_pairs={{0,1},{1,2},{2,3},{3,4},{4,5},{5,6},{6,7},{7,8},{8,9},{9,10},{10,1... | collective-permute-start | bytes 2359304 | tf_op jit(solution)/shard_map/while/body/eval_jaxpr/ppermute | solution.py:9
  169.8 19.6 %collective-permute-start = (s32[768]{0:T(1024)S(1)}, s32[768]{0:T(1024)S(1)}, u32[]{:S(2)}, u32[]{:S(2)}) collective-permute-start(s32[768]{0:T(1024)S(1)} %get-tuple-element.175), channel_id=1, source_target_pairs={{0,1},{1,2},{2,3},{3,4},{4,5},{5,6},{6,7},{7,8},{8,9},{9,10},{10,1... | collective-permute-start | bytes 9224 | tf_op jit(solution)/shard_map/while/body/eval_jaxpr/ppermute | solution.py:9
  169.9 19.5 %collective-permute-start.1 = (s32[768]{0:T(1024)S(1)}, s32[768]{0:T(1024)S(1)}, u32[]{:S(2)}, u32[]{:S(2)}) collective-permute-start(s32[768]{0:T(1024)S(1)} %get-tuple-element.174), channel_id=1, source_target_pairs={{0,1},{1,2},{2,3},{3,4},{4,5},{5,6},{6,7},{7,8},{8,9},{9,10},{10,1... | collective-permute-start | bytes 9224 | tf_op jit(solution)/shard_map/while/body/eval_jaxpr/ppermute | solution.py:9
  190.5 18.7 %collective-permute-start.2 = (bf16[768,512]{1,0:T(8,128)(2,1)S(1)}, bf16[768,512]{1,0:T(8,128)(2,1)S(1)}, u32[]{:S(2)}, u32[]{:S(2)}) collective-permute-start(bf16[768,512]{1,0:T(8,128)(2,1)S(1)} %get-tuple-element.173), channel_id=1, source_target_pairs={{0,1},{1,2},{2,3},{3,4},{4,5},{5,6},{6,7},{7,8},{8,9},{9,10},{10,1... | collective-permute-start | bytes 2359304 | tf_op jit(solution)/shard_map/while/body/eval_jaxpr/ppermute | solution.py:9
  190.6 18.6 %collective-permute-start = (s32[768]{0:T(1024)S(1)}, s32[768]{0:T(1024)S(1)}, u32[]{:S(2)}, u32[]{:S(2)}) collective-permute-start(s32[768]{0:T(1024)S(1)} %get-tuple-element.175), channel_id=1, source_target_pairs={{0,1},{1,2},{2,3},{3,4},{4,5},{5,6},{6,7},{7,8},{8,9},{9,10},{10,1... | collective-permute-start | bytes 9224 | tf_op jit(solution)/shard_map/while/body/eval_jaxpr/ppermute | solution.py:9
  190.7 18.5 %collective-permute-start.1 = (s32[768]{0:T(1024)S(1)}, s32[768]{0:T(1024)S(1)}, u32[]{:S(2)}, u32[]{:S(2)}) collective-permute-start(s32[768]{0:T(1024)S(1)} %get-tuple-element.174), channel_id=1, source_target_pairs={{0,1},{1,2},{2,3},{3,4},{4,5},{5,6},{6,7},{7,8},{8,9},{9,10},{10,1... | collective-permute-start | bytes 9224 | tf_op jit(solution)/shard_map/while/body/eval_jaxpr/ppermute | solution.py:9
  210.4 17.8 %collective-permute-start.2 = (bf16[768,512]{1,0:T(8,128)(2,1)S(1)}, bf16[768,512]{1,0:T(8,128)(2,1)S(1)}, u32[]{:S(2)}, u32[]{:S(2)}) collective-permute-start(bf16[768,512]{1,0:T(8,128)(2,1)S(1)} %get-tuple-element.173), channel_id=1, source_target_pairs={{0,1},{1,2},{2,3},{3,4},{4,5},{5,6},{6,7},{7,8},{8,9},{9,10},{10,1... | collective-permute-start | bytes 2359304 | tf_op jit(solution)/shard_map/while/body/eval_jaxpr/ppermute | solution.py:9
  210.5 17.7 %collective-permute-start = (s32[768]{0:T(1024)S(1)}, s32[768]{0:T(1024)S(1)}, u32[]{:S(2)}, u32[]{:S(2)}) collective-permute-start(s32[768]{0:T(1024)S(1)} %get-tuple-element.175), channel_id=1, source_target_pairs={{0,1},{1,2},{2,3},{3,4},{4,5},{5,6},{6,7},{7,8},{8,9},{9,10},{10,1... | collective-permute-start | bytes 9224 | tf_op jit(solution)/shard_map/while/body/eval_jaxpr/ppermute | solution.py:9
  210.6 17.6 %collective-permute-start.1 = (s32[768]{0:T(1024)S(1)}, s32[768]{0:T(1024)S(1)}, u32[]{:S(2)}, u32[]{:S(2)}) collective-permute-start(s32[768]{0:T(1024)S(1)} %get-tuple-element.174), channel_id=1, source_target_pairs={{0,1},{1,2},{2,3},{3,4},{4,5},{5,6},{6,7},{7,8},{8,9},{9,10},{10,1... | collective-permute-start | bytes 9224 | tf_op jit(solution)/shard_map/while/body/eval_jaxpr/ppermute | solution.py:9
  229.4 16.9 %collective-permute-start.2 = (bf16[768,512]{1,0:T(8,128)(2,1)S(1)}, bf16[768,512]{1,0:T(8,128)(2,1)S(1)}, u32[]{:S(2)}, u32[]{:S(2)}) collective-permute-start(bf16[768,512]{1,0:T(8,128)(2,1)S(1)} %get-tuple-element.173), channel_id=1, source_target_pairs={{0,1},{1,2},{2,3},{3,4},{4,5},{5,6},{6,7},{7,8},{8,9},{9,10},{10,1... | collective-permute-start | bytes 2359304 | tf_op jit(solution)/shard_map/while/body/eval_jaxpr/ppermute | solution.py:9
  229.4 16.8 %collective-permute-start = (s32[768]{0:T(1024)S(1)}, s32[768]{0:T(1024)S(1)}, u32[]{:S(2)}, u32[]{:S(2)}) collective-permute-start(s32[768]{0:T(1024)S(1)} %get-tuple-element.175), channel_id=1, source_target_pairs={{0,1},{1,2},{2,3},{3,4},{4,5},{5,6},{6,7},{7,8},{8,9},{9,10},{10,1... | collective-permute-start | bytes 9224 | tf_op jit(solution)/shard_map/while/body/eval_jaxpr/ppermute | solution.py:9
  229.5 16.7 %collective-permute-start.1 = (s32[768]{0:T(1024)S(1)}, s32[768]{0:T(1024)S(1)}, u32[]{:S(2)}, u32[]{:S(2)}) collective-permute-start(s32[768]{0:T(1024)S(1)} %get-tuple-element.174), channel_id=1, source_target_pairs={{0,1},{1,2},{2,3},{3,4},{4,5},{5,6},{6,7},{7,8},{8,9},{9,10},{10,1... | collective-permute-start | bytes 9224 | tf_op jit(solution)/shard_map/while/body/eval_jaxpr/ppermute | solution.py:9
  247.4 16.0 %collective-permute-start.2 = (bf16[768,512]{1,0:T(8,128)(2,1)S(1)}, bf16[768,512]{1,0:T(8,128)(2,1)S(1)}, u32[]{:S(2)}, u32[]{:S(2)}) collective-permute-start(bf16[768,512]{1,0:T(8,128)(2,1)S(1)} %get-tuple-element.173), channel_id=1, source_target_pairs={{0,1},{1,2},{2,3},{3,4},{4,5},{5,6},{6,7},{7,8},{8,9},{9,10},{10,1... | collective-permute-start | bytes 2359304 | tf_op jit(solution)/shard_map/while/body/eval_jaxpr/ppermute | solution.py:9
  247.5 15.9 %collective-permute-start = (s32[768]{0:T(1024)S(1)}, s32[768]{0:T(1024)S(1)}, u32[]{:S(2)}, u32[]{:S(2)}) collective-permute-start(s32[768]{0:T(1024)S(1)} %get-tuple-element.175), channel_id=1, source_target_pairs={{0,1},{1,2},{2,3},{3,4},{4,5},{5,6},{6,7},{7,8},{8,9},{9,10},{10,1... | collective-permute-start | bytes 9224 | tf_op jit(solution)/shard_map/while/body/eval_jaxpr/ppermute | solution.py:9
  247.6 15.8 %collective-permute-start.1 = (s32[768]{0:T(1024)S(1)}, s32[768]{0:T(1024)S(1)}, u32[]{:S(2)}, u32[]{:S(2)}) collective-permute-start(s32[768]{0:T(1024)S(1)} %get-tuple-element.174), channel_id=1, source_target_pairs={{0,1},{1,2},{2,3},{3,4},{4,5},{5,6},{6,7},{7,8},{8,9},{9,10},{10,1... | collective-permute-start | bytes 9224 | tf_op jit(solution)/shard_map/while/body/eval_jaxpr/ppermute | solution.py:9
  264.5 15.0 %collective-permute-start.2 = (bf16[768,512]{1,0:T(8,128)(2,1)S(1)}, bf16[768,512]{1,0:T(8,128)(2,1)S(1)}, u32[]{:S(2)}, u32[]{:S(2)}) collective-permute-start(bf16[768,512]{1,0:T(8,128)(2,1)S(1)} %get-tuple-element.173), channel_id=1, source_target_pairs={{0,1},{1,2},{2,3},{3,4},{4,5},{5,6},{6,7},{7,8},{8,9},{9,10},{10,1... | collective-permute-start | bytes 2359304 | tf_op jit(solution)/shard_map/while/body/eval_jaxpr/ppermute | solution.py:9
  264.6 14.9 %collective-permute-start = (s32[768]{0:T(1024)S(1)}, s32[768]{0:T(1024)S(1)}, u32[]{:S(2)}, u32[]{:S(2)}) collective-permute-start(s32[768]{0:T(1024)S(1)} %get-tuple-element.175), channel_id=1, source_target_pairs={{0,1},{1,2},{2,3},{3,4},{4,5},{5,6},{6,7},{7,8},{8,9},{9,10},{10,1... | collective-permute-start | bytes 9224 | tf_op jit(solution)/shard_map/while/body/eval_jaxpr/ppermute | solution.py:9
  264.7 14.9 %collective-permute-start.1 = (s32[768]{0:T(1024)S(1)}, s32[768]{0:T(1024)S(1)}, u32[]{:S(2)}, u32[]{:S(2)}) collective-permute-start(s32[768]{0:T(1024)S(1)} %get-tuple-element.174), channel_id=1, source_target_pairs={{0,1},{1,2},{2,3},{3,4},{4,5},{5,6},{6,7},{7,8},{8,9},{9,10},{10,1... | collective-permute-start | bytes 9224 | tf_op jit(solution)/shard_map/while/body/eval_jaxpr/ppermute | solution.py:9
  280.7 15.0 %collective-permute-start.2 = (bf16[768,512]{1,0:T(8,128)(2,1)S(1)}, bf16[768,512]{1,0:T(8,128)(2,1)S(1)}, u32[]{:S(2)}, u32[]{:S(2)}) collective-permute-start(bf16[768,512]{1,0:T(8,128)(2,1)S(1)} %get-tuple-element.173), channel_id=1, source_target_pairs={{0,1},{1,2},{2,3},{3,4},{4,5},{5,6},{6,7},{7,8},{8,9},{9,10},{10,1... | collective-permute-start | bytes 2359304 | tf_op jit(solution)/shard_map/while/body/eval_jaxpr/ppermute | solution.py:9
  280.8 14.9 %collective-permute-start = (s32[768]{0:T(1024)S(1)}, s32[768]{0:T(1024)S(1)}, u32[]{:S(2)}, u32[]{:S(2)}) collective-permute-start(s32[768]{0:T(1024)S(1)} %get-tuple-element.175), channel_id=1, source_target_pairs={{0,1},{1,2},{2,3},{3,4},{4,5},{5,6},{6,7},{7,8},{8,9},{9,10},{10,1... | collective-permute-start | bytes 9224 | tf_op jit(solution)/shard_map/while/body/eval_jaxpr/ppermute | solution.py:9
  280.9 14.8 %collective-permute-start.1 = (s32[768]{0:T(1024)S(1)}, s32[768]{0:T(1024)S(1)}, u32[]{:S(2)}, u32[]{:S(2)}) collective-permute-start(s32[768]{0:T(1024)S(1)} %get-tuple-element.174), channel_id=1, source_target_pairs={{0,1},{1,2},{2,3},{3,4},{4,5},{5,6},{6,7},{7,8},{8,9},{9,10},{10,1... | collective-permute-start | bytes 9224 | tf_op jit(solution)/shard_map/while/body/eval_jaxpr/ppermute | solution.py:9
  296.9 14.8 %collective-permute-start.2 = (bf16[768,512]{1,0:T(8,128)(2,1)S(1)}, bf16[768,512]{1,0:T(8,128)(2,1)S(1)}, u32[]{:S(2)}, u32[]{:S(2)}) collective-permute-start(bf16[768,512]{1,0:T(8,128)(2,1)S(1)} %get-tuple-element.173), channel_id=1, source_target_pairs={{0,1},{1,2},{2,3},{3,4},{4,5},{5,6},{6,7},{7,8},{8,9},{9,10},{10,1... | collective-permute-start | bytes 2359304 | tf_op jit(solution)/shard_map/while/body/eval_jaxpr/ppermute | solution.py:9
  296.9 14.7 %collective-permute-start = (s32[768]{0:T(1024)S(1)}, s32[768]{0:T(1024)S(1)}, u32[]{:S(2)}, u32[]{:S(2)}) collective-permute-start(s32[768]{0:T(1024)S(1)} %get-tuple-element.175), channel_id=1, source_target_pairs={{0,1},{1,2},{2,3},{3,4},{4,5},{5,6},{6,7},{7,8},{8,9},{9,10},{10,1... | collective-permute-start | bytes 9224 | tf_op jit(solution)/shard_map/while/body/eval_jaxpr/ppermute | solution.py:9
  297.0 14.6 %collective-permute-start.1 = (s32[768]{0:T(1024)S(1)}, s32[768]{0:T(1024)S(1)}, u32[]{:S(2)}, u32[]{:S(2)}) collective-permute-start(s32[768]{0:T(1024)S(1)} %get-tuple-element.174), channel_id=1, source_target_pairs={{0,1},{1,2},{2,3},{3,4},{4,5},{5,6},{6,7},{7,8},{8,9},{9,10},{10,1... | collective-permute-start | bytes 9224 | tf_op jit(solution)/shard_map/while/body/eval_jaxpr/ppermute | solution.py:9
  312.8 15.9 %collective-permute-start.2 = (bf16[768,512]{1,0:T(8,128)(2,1)S(1)}, bf16[768,512]{1,0:T(8,128)(2,1)S(1)}, u32[]{:S(2)}, u32[]{:S(2)}) collective-permute-start(bf16[768,512]{1,0:T(8,128)(2,1)S(1)} %get-tuple-element.173), channel_id=1, source_target_pairs={{0,1},{1,2},{2,3},{3,4},{4,5},{5,6},{6,7},{7,8},{8,9},{9,10},{10,1... | collective-permute-start | bytes 2359304 | tf_op jit(solution)/shard_map/while/body/eval_jaxpr/ppermute | solution.py:9
  312.9 15.8 %collective-permute-start = (s32[768]{0:T(1024)S(1)}, s32[768]{0:T(1024)S(1)}, u32[]{:S(2)}, u32[]{:S(2)}) collective-permute-start(s32[768]{0:T(1024)S(1)} %get-tuple-element.175), channel_id=1, source_target_pairs={{0,1},{1,2},{2,3},{3,4},{4,5},{5,6},{6,7},{7,8},{8,9},{9,10},{10,1... | collective-permute-start | bytes 9224 | tf_op jit(solution)/shard_map/while/body/eval_jaxpr/ppermute | solution.py:9
  313.0 15.7 %collective-permute-start.1 = (s32[768]{0:T(1024)S(1)}, s32[768]{0:T(1024)S(1)}, u32[]{:S(2)}, u32[]{:S(2)}) collective-permute-start(s32[768]{0:T(1024)S(1)} %get-tuple-element.174), channel_id=1, source_target_pairs={{0,1},{1,2},{2,3},{3,4},{4,5},{5,6},{6,7},{7,8},{8,9},{9,10},{10,1... | collective-permute-start | bytes 9224 | tf_op jit(solution)/shard_map/while/body/eval_jaxpr/ppermute | solution.py:9
  329.9 17.0 %collective-permute-start.2 = (bf16[768,512]{1,0:T(8,128)(2,1)S(1)}, bf16[768,512]{1,0:T(8,128)(2,1)S(1)}, u32[]{:S(2)}, u32[]{:S(2)}) collective-permute-start(bf16[768,512]{1,0:T(8,128)(2,1)S(1)} %get-tuple-element.173), channel_id=1, source_target_pairs={{0,1},{1,2},{2,3},{3,4},{4,5},{5,6},{6,7},{7,8},{8,9},{9,10},{10,1... | collective-permute-start | bytes 2359304 | tf_op jit(solution)/shard_map/while/body/eval_jaxpr/ppermute | solution.py:9
  330.0 16.9 %collective-permute-start = (s32[768]{0:T(1024)S(1)}, s32[768]{0:T(1024)S(1)}, u32[]{:S(2)}, u32[]{:S(2)}) collective-permute-start(s32[768]{0:T(1024)S(1)} %get-tuple-element.175), channel_id=1, source_target_pairs={{0,1},{1,2},{2,3},{3,4},{4,5},{5,6},{6,7},{7,8},{8,9},{9,10},{10,1... | collective-permute-start | bytes 9224 | tf_op jit(solution)/shard_map/while/body/eval_jaxpr/ppermute | solution.py:9
  330.0 16.8 %collective-permute-start.1 = (s32[768]{0:T(1024)S(1)}, s32[768]{0:T(1024)S(1)}, u32[]{:S(2)}, u32[]{:S(2)}) collective-permute-start(s32[768]{0:T(1024)S(1)} %get-tuple-element.174), channel_id=1, source_target_pairs={{0,1},{1,2},{2,3},{3,4},{4,5},{5,6},{6,7},{7,8},{8,9},{9,10},{10,1... | collective-permute-start | bytes 9224 | tf_op jit(solution)/shard_map/while/body/eval_jaxpr/ppermute | solution.py:9
  348.0 18.1 %collective-permute-start.2 = (bf16[768,512]{1,0:T(8,128)(2,1)S(1)}, bf16[768,512]{1,0:T(8,128)(2,1)S(1)}, u32[]{:S(2)}, u32[]{:S(2)}) collective-permute-start(bf16[768,512]{1,0:T(8,128)(2,1)S(1)} %get-tuple-element.173), channel_id=1, source_target_pairs={{0,1},{1,2},{2,3},{3,4},{4,5},{5,6},{6,7},{7,8},{8,9},{9,10},{10,1... | collective-permute-start | bytes 2359304 | tf_op jit(solution)/shard_map/while/body/eval_jaxpr/ppermute | solution.py:9
  348.1 18.0 %collective-permute-start = (s32[768]{0:T(1024)S(1)}, s32[768]{0:T(1024)S(1)}, u32[]{:S(2)}, u32[]{:S(2)}) collective-permute-start(s32[768]{0:T(1024)S(1)} %get-tuple-element.175), channel_id=1, source_target_pairs={{0,1},{1,2},{2,3},{3,4},{4,5},{5,6},{6,7},{7,8},{8,9},{9,10},{10,1... | collective-permute-start | bytes 9224 | tf_op jit(solution)/shard_map/while/body/eval_jaxpr/ppermute | solution.py:9
  348.2 17.9 %collective-permute-start.1 = (s32[768]{0:T(1024)S(1)}, s32[768]{0:T(1024)S(1)}, u32[]{:S(2)}, u32[]{:S(2)}) collective-permute-start(s32[768]{0:T(1024)S(1)} %get-tuple-element.174), channel_id=1, source_target_pairs={{0,1},{1,2},{2,3},{3,4},{4,5},{5,6},{6,7},{7,8},{8,9},{9,10},{10,1... | collective-permute-start | bytes 9224 | tf_op jit(solution)/shard_map/while/body/eval_jaxpr/ppermute | solution.py:9
  367.2 19.2 %collective-permute-start.2 = (bf16[768,512]{1,0:T(8,128)(2,1)S(1)}, bf16[768,512]{1,0:T(8,128)(2,1)S(1)}, u32[]{:S(2)}, u32[]{:S(2)}) collective-permute-start(bf16[768,512]{1,0:T(8,128)(2,1)S(1)} %get-tuple-element.173), channel_id=1, source_target_pairs={{0,1},{1,2},{2,3},{3,4},{4,5},{5,6},{6,7},{7,8},{8,9},{9,10},{10,1... | collective-permute-start | bytes 2359304 | tf_op jit(solution)/shard_map/while/body/eval_jaxpr/ppermute | solution.py:9
  367.3 19.1 %collective-permute-start = (s32[768]{0:T(1024)S(1)}, s32[768]{0:T(1024)S(1)}, u32[]{:S(2)}, u32[]{:S(2)}) collective-permute-start(s32[768]{0:T(1024)S(1)} %get-tuple-element.175), channel_id=1, source_target_pairs={{0,1},{1,2},{2,3},{3,4},{4,5},{5,6},{6,7},{7,8},{8,9},{9,10},{10,1... | collective-permute-start | bytes 9224 | tf_op jit(solution)/shard_map/while/body/eval_jaxpr/ppermute | solution.py:9
  367.4 19.0 %collective-permute-start.1 = (s32[768]{0:T(1024)S(1)}, s32[768]{0:T(1024)S(1)}, u32[]{:S(2)}, u32[]{:S(2)}) collective-permute-start(s32[768]{0:T(1024)S(1)} %get-tuple-element.174), channel_id=1, source_target_pairs={{0,1},{1,2},{2,3},{3,4},{4,5},{5,6},{6,7},{7,8},{8,9},{9,10},{10,1... | collective-permute-start | bytes 9224 | tf_op jit(solution)/shard_map/while/body/eval_jaxpr/ppermute | solution.py:9
  387.6 20.2 %collective-permute-start.2 = (bf16[768,512]{1,0:T(8,128)(2,1)S(1)}, bf16[768,512]{1,0:T(8,128)(2,1)S(1)}, u32[]{:S(2)}, u32[]{:S(2)}) collective-permute-start(bf16[768,512]{1,0:T(8,128)(2,1)S(1)} %get-tuple-element.173), channel_id=1, source_target_pairs={{0,1},{1,2},{2,3},{3,4},{4,5},{5,6},{6,7},{7,8},{8,9},{9,10},{10,1... | collective-permute-start | bytes 2359304 | tf_op jit(solution)/shard_map/while/body/eval_jaxpr/ppermute | solution.py:9
  387.6 20.1 %collective-permute-start = (s32[768]{0:T(1024)S(1)}, s32[768]{0:T(1024)S(1)}, u32[]{:S(2)}, u32[]{:S(2)}) collective-permute-start(s32[768]{0:T(1024)S(1)} %get-tuple-element.175), channel_id=1, source_target_pairs={{0,1},{1,2},{2,3},{3,4},{4,5},{5,6},{6,7},{7,8},{8,9},{9,10},{10,1... | collective-permute-start | bytes 9224 | tf_op jit(solution)/shard_map/while/body/eval_jaxpr/ppermute | solution.py:9
  387.7 20.0 %collective-permute-start.1 = (s32[768]{0:T(1024)S(1)}, s32[768]{0:T(1024)S(1)}, u32[]{:S(2)}, u32[]{:S(2)}) collective-permute-start(s32[768]{0:T(1024)S(1)} %get-tuple-element.174), channel_id=1, source_target_pairs={{0,1},{1,2},{2,3},{3,4},{4,5},{5,6},{6,7},{7,8},{8,9},{9,10},{10,1... | collective-permute-start | bytes 9224 | tf_op jit(solution)/shard_map/while/body/eval_jaxpr/ppermute | solution.py:9
  408.9 21.3 %collective-permute-start.2 = (bf16[768,512]{1,0:T(8,128)(2,1)S(1)}, bf16[768,512]{1,0:T(8,128)(2,1)S(1)}, u32[]{:S(2)}, u32[]{:S(2)}) collective-permute-start(bf16[768,512]{1,0:T(8,128)(2,1)S(1)} %get-tuple-element.173), channel_id=1, source_target_pairs={{0,1},{1,2},{2,3},{3,4},{4,5},{5,6},{6,7},{7,8},{8,9},{9,10},{10,1... | collective-permute-start | bytes 2359304 | tf_op jit(solution)/shard_map/while/body/eval_jaxpr/ppermute | solution.py:9
  409.0 21.2 %collective-permute-start = (s32[768]{0:T(1024)S(1)}, s32[768]{0:T(1024)S(1)}, u32[]{:S(2)}, u32[]{:S(2)}) collective-permute-start(s32[768]{0:T(1024)S(1)} %get-tuple-element.175), channel_id=1, source_target_pairs={{0,1},{1,2},{2,3},{3,4},{4,5},{5,6},{6,7},{7,8},{8,9},{9,10},{10,1... | collective-permute-start | bytes 9224 | tf_op jit(solution)/shard_map/while/body/eval_jaxpr/ppermute | solution.py:9
  409.1 21.1 %collective-permute-start.1 = (s32[768]{0:T(1024)S(1)}, s32[768]{0:T(1024)S(1)}, u32[]{:S(2)}, u32[]{:S(2)}) collective-permute-start(s32[768]{0:T(1024)S(1)} %get-tuple-element.174), channel_id=1, source_target_pairs={{0,1},{1,2},{2,3},{3,4},{4,5},{5,6},{6,7},{7,8},{8,9},{9,10},{10,1... | collective-permute-start | bytes 9224 | tf_op jit(solution)/shard_map/while/body/eval_jaxpr/ppermute | solution.py:9
  (4 other events, 147.8 us)
where the time goes:
time: 462 us; the launch traced here: 459 us
  waiting for transfers between devices  270 us (58%)
  local copies, waits for them, and re-layouts  110 us (24%)
  starting transfers between devices  33.1 us (7%)
  blocking collectives  25.2 us (5%)
  matrix products  16.7 us (4%)
    ppermute x45, waiting for transfers between devices, from_behind(): return lax.ppermute(x, axis, [(i, (i + by) % size) for i in range(size)])  258 us
    scatter x1, local copies, waits for them, and re-layouts, body(): jnp.zeros((groups, capacity), jnp.int32).at[target, slot].set(order)  35.4 us
    scatter x1, local copies, waits for them, and re-layouts, body(): jnp.full((groups, capacity), -1, jnp.int32).at[target, slot].set(cluster)  35.3 us
    scatter x1, local copies, waits for them, and re-layouts, body(): jnp.zeros((groups, capacity, width), jnp.bfloat16).at[target, slot]  32.6 us
    all_to_all x1, blocking collectives, body(): lax.all_to_all(best.reshape(groups, capacity), 'grp', split_axis=0, conca...  25.2 us
    dot_general x16, matrix products, fold_block(): lax.dot_general(local_unit, block_unit, (((1,), (1,)), ((), ())), preferr...  16.7 us
    all_to_all x1, waiting for transfers between devices, body(): lax.all_to_all(send_unit, 'grp', split_axis=0, concat_axis=0, tiled=True)  12 us
    ppermute x45, starting transfers between devices, from_behind(): return lax.ppermute(x, axis, [(i, (i + by) % size) for i in range(size)])  10.2 us
  transfers between devices with their start and end apart: 48, of which 16 were waited for; matrix products, arithmetic and copies ran while one was open for 16% of the time, Pallas kernels for 0%

commit v1 on v0

v1 whole, which is shorter than its diff:
```python
import jax
import jax.numpy as jnp
from jax import lax
from jax.experimental import pallas as pl
from jax.experimental.pallas import tpu as pltpu
from jax.sharding import PartitionSpec as P

MESH = pl.DeviceIdType.MESH
ROWS, WIDTH, HEAD = 256, 512, 16
TALL = ROWS + HEAD
CHUNKS = ((0, 80), (80, 64), (144, 64), (208, 64))
RING = 8
SLOTS = [(0, 0, z) for z in range(8)] + [
    (1, 0, 0), (0, 3, 0), (2, 0, 0), (1, 3, 0), (3, 3, 0), (0, 2, 0), (2, 1, 0), (3, 2, 0), (2, 2, 0),
]
STEP = {"+x": (1, 0, 0), "-x": (3, 0, 0), "+y": (0, 1, 0), "-y": (0, 3, 0), "+z": (0, 0, 1), "-z": (0, 0, 7)}
TREE = {
    (0, 0, 1): ((0, 0, 0), "+z"), (0, 0, 2): ((0, 0, 1), "+z"), (0, 0, 3): ((0, 0, 2), "+z"),
    (0, 0, 7): ((0, 0, 0), "-z"), (0, 0, 6): ((0, 0, 7), "-z"), (0, 0, 5): ((0, 0, 6), "-z"),
    (0, 0, 4): (((0, 0, 3), "+z"), ((0, 0, 5), "-z")),
    (1, 0, 0): ((0, 0, 0), "+x"), (0, 3, 0): ((0, 0, 0), "-y"), (2, 0, 0): ((1, 0, 0), "+x"),
    (1, 3, 0): ((0, 3, 0), "+x"), (3, 3, 0): ((0, 3, 0), "-x"), (0, 2, 0): ((0, 3, 0), "-y"),
    (2, 1, 0): ((2, 0, 0), "+y"), (3, 2, 0): ((3, 3, 0), "-y"), (2, 2, 0): ((3, 2, 0), "-x"),
}
NS = len(SLOTS)
NC = len(CHUNKS)
WRAP = (4, 4, 8)


def plus(a, b):
    return tuple((p + q) % w for p, q, w in zip(a, b, WRAP))


def minus(a):
    return tuple((-p) % w for p, w in zip(a, WRAP))


def edges():
    out = {}
    for s in range(1, NS):
        for c in range(NC):
            t = TREE[SLOTS[s]]
            if not isinstance(t[1], str):
                t = t[c % 2]
            out[s, c] = (SLOTS.index(t[0]), t[1])
            assert plus(t[0], STEP[t[1]]) == SLOTS[s]
    return out


EDGE = edges()
KIDS = {}
for (s_, c_), (p_, u_) in EDGE.items():
    KIDS.setdefault((p_, c_), []).append((s_, u_))


def arrivals(block=4.8, hop=2.2):
    need = {}
    for s, c in EDGE:
        n, k = 0, (s, c)
        while k[0]:
            n, k = n + 1, (EDGE[k][0], c)
        need[s, c] = n
    tall = {k: 0 for k in EDGE}
    for s, c in EDGE:
        k = (s, c)
        while k[0]:
            tall[k] = max(tall[k], need[s, c] - need[k])
            k = (EDGE[k][0], c)
    at = {(0, c): 0.0 for c in range(NC)}
    free = {u: 0.0 for u in STEP}
    left = set(EDGE)
    while left:
        ready = [
            (max(at[EDGE[k][0], k[1]], free[EDGE[k][1]]), -tall[k], k[1], k[0]) for k in left if (EDGE[k][0], k[1]) in at
        ]
        t, _, c, s = min(ready)
        free[EDGE[s, c][1]] = t + block / NC
        at[s, c] = t + block / NC + hop
        left.remove((s, c))
    return at


HALF_TURN = [s for s in range(RING, NS) if plus(SLOTS[s], SLOTS[s]) == (0, 0, 0)]


def pair_tasks():
    out = [(0, a) for a in (1, 2, 3)]
    for s in range(RING, NS):
        out += [(s, a) for a in ((1, 2, 3) if s in HALF_TURN else range(RING))]
    return out


HOME = [(s, 0) for s in range(RING, NS)] + [(a, f) for a in range(1, RING) for f in (0, 1)] + [(0, 1)]


def plan():
    at = arrivals()
    seen = sorted((t, s, c) for (s, c), t in at.items() if s)
    whole = {s: max(at[s, c] for c in range(NC)) for s in range(NS)}
    ready = {t: max(whole[t[0]], whole[t[1]] + 1.5) for t in pair_tasks()}
    halves = {(s, a): max(whole[s], whole[a] + 1.5) for s in HALF_TURN for a in (0, 4)}
    halves[0, 4] = whole[4] + 1.5
    todo = sorted(ready, key=lambda t: ready[t])
    steps, now = [], 0.0
    left_h = sorted(halves, key=lambda t: halves[t])
    while todo or left_h:
        while seen and seen[0][0] <= now:
            _, s, c = seen.pop(0)
            steps.append(("chunk", s, c))
        able = [t for t in todo if ready[t] <= now][:4]
        if len(able) % 2 and len(able) > 1:
            able = able[:-1]
        if len(able) >= 2:
            steps.append(("tasks", able))
            todo = [t for t in todo if t not in able]
            now += 0.28 * len(able)
        elif left_h and halves[left_h[0]] <= now:
            steps.append(("half", left_h.pop(0)))
            now += 0.25
        elif not seen and len(able) == 1:
            steps.append(("tasks", able))
            todo = [t for t in todo if t not in able]
            now += 0.3
        elif seen:
            now = seen[0][0]
        else:
            now += 0.25
    return steps


def pick(table, i):
    value = jnp.int32(table[-1])
    for k in range(len(table) - 2, -1, -1):
        if table[k] != table[-1]:
            value = jnp.where(i == k, jnp.int32(table[k]), value)
    return value


def kernel(x_ref, cl_ref, ord_ref, out_ref, buf, row_cl, row_ord, col_cl, col_ord, row_best, col_best, score,
           send_back, got_back, link_out, link_in, pair_out, pair_in, home_out, home_in):
    g, b = lax.axis_index("grp"), lax.axis_index("blk")
    core = g % 2
    here = (g // 4, ((g // 2) % 2) * 2 + b // 8, b % 8)

    def device(d, flip=0):
        x, y, z = ((h + k) % w for h, k, w in zip(here, d, WRAP))
        return ((x * 2 + y // 2) * 2 + (1 - core if flip else core), (y % 2) * 8 + z)

    goes = {(minus(STEP[u]), 0) for u in STEP} | {((0, 0, 0), 1)} | {(SLOTS[s], f) for s, f in HOME}
    comes = {(minus(d), f) for d, f in goes}
    barrier = pltpu.get_barrier_semaphore()
    for d, f in sorted(comes):
        pl.semaphore_signal(barrier, inc=1, device_id=device(d, f), device_id_type=MESH)

    values = x_ref[...].astype(jnp.float32)
    scale = lax.rsqrt(jnp.sum(values * values, axis=1, keepdims=True) + 1e-06)
    buf[0, 0, pl.ds(HEAD, ROWS), :] = (values * scale).astype(jnp.bfloat16)
    line = lax.broadcasted_iota(jnp.int32, (HEAD, ROWS), 0)
    rank = ord_ref[...]
    head = jnp.where(line == 0, cl_ref[...], jnp.where(line == 1, rank // 256, jnp.where(line == 2, rank % 256, 0)))
    head = head.astype(jnp.float32).astype(jnp.bfloat16)
    buf[0, 0, pl.ds(0, HEAD), pl.ds(0, ROWS)] = head
    buf[0, 0, pl.ds(0, HEAD), pl.ds(ROWS, WIDTH - ROWS)] = jnp.zeros((HEAD, WIDTH - ROWS), jnp.bfloat16)

    pl.semaphore_wait(barrier, len(goes))

    def hop(s, c):
        lo, n = CHUNKS[c]
        p, u = EDGE[s, c]
        return pltpu.make_async_remote_copy(
            src_ref=buf.at[0, p, pl.ds(lo, n)], dst_ref=buf.at[0, s, pl.ds(lo, n)],
            send_sem=link_out.at[s, c], recv_sem=link_in.at[s, c],
            device_id=device(minus(STEP[u])), device_id_type=MESH,
        )

    def across(a):
        return pltpu.make_async_remote_copy(
            src_ref=buf.at[0, a], dst_ref=buf.at[1, a], send_sem=pair_out.at[a], recv_sem=pair_in.at[a],
            device_id=device((0, 0, 0), 1), device_id_type=MESH,
        )

    for c in range(NC):
        for s, _ in KIDS[0, c]:
            hop(s, c).start()
    across(0).start()

    def row_slot(s):
        return 0 if s == 0 else s - RING + 1

    rows16 = lax.broadcasted_iota(jnp.int32, (HEAD, 256), 0)
    lane16 = lax.broadcasted_iota(jnp.int32, (HEAD, 256), 1)
    spread = jnp.where(
        lane16 < 128, jnp.where(rows16 == 0, 1.0, 0.0), jnp.where(rows16 == 1, 256.0, jnp.where(rows16 == 2, 1.0, 0.0))
    ).astype(jnp.bfloat16)

    def row_side(s):
        wide = lax.dot_general(
            buf[0, s, pl.ds(0, HEAD), pl.ds(0, ROWS)], spread, (((0,), (0,)), ((), ())), preferred_element_type=jnp.float32
        )
        k = row_slot(s)
        row_cl[k] = wide[:, :128]
        row_ord[k] = wide[:, 128:]

    def col_side(a, half):
        top = buf[half, a, pl.ds(0, HEAD), pl.ds(0, ROWS)].astype(jnp.float32)
        col_cl[a, half] = jnp.broadcast_to(top[0:1], (8, ROWS))
        col_ord[a, half] = jnp.broadcast_to(top[1:2] * 256.0 + top[2:3], (8, ROWS))

    row_best[...] = jnp.full(row_best.shape, -1.0, jnp.float32)
    col_best[...] = jnp.full(col_best.shape, -1.0, jnp.float32)

    def dot(s, a):
        rows = buf[0, s, pl.ds(HEAD, ROWS), :]
        columns = jnp.concatenate([buf[h, a, pl.ds(HEAD, ROWS), :] for h in (0, 1)], axis=0)
        return lax.dot_general(rows, columns, (((1,), (1,)), ((), ())), preferred_element_type=jnp.float32)

    def fold(ref, k, a, halves=(0, 1), both=True):
        tiles = [(h, t) for h in halves for t in (0, 128)]
        cl = [col_cl[a, h, :, pl.ds(t, 128)] for h, t in tiles]
        rk = [col_ord[a, h, :, pl.ds(t, 128)] for h, t in tiles]
        top = [col_best[a, h, :, pl.ds(t, 128)] for h, t in tiles] if both else None
        for i in range(ROWS // 8):
            at = pl.ds(8 * i, 8)
            mine, rank, best = row_cl[k, at, :], row_ord[k, at, :], row_best[k, at, :]
            for n in range(len(tiles)):
                s = ref[at, pl.ds(128 * n, 128)]
                same = jnp.where(mine == cl[n], s, -1.0)
                later = rk[n] < rank
                best = jnp.maximum(best, jnp.where(later, same, -1.0))
                if both:
                    top[n] = jnp.maximum(top[n], jnp.where(later, -1.0, same))
            row_best[k, at, :] = best
        if both:
            for n, (h, t) in enumerate(tiles):
                col_best[a, h, :, pl.ds(t, 128)] = top[n]

    row_side(0)
    col_side(0, 0)
    met = {0}

    def meet(a):
        if ("pair", a) not in met:
            met.add(("pair", a))
            across(a).wait_recv()
            col_side(a, 1)

    def flip(s):
        d = SLOTS[s]
        return here[0] // 2 if d[0] == 2 else (here[1] // 2 if d[1] == 2 else here[2] // 4)

    meet(0)
    score[0] = dot(0, 0)
    fold(score.at[0], 0, 0, both=False)

    parts = {s: 0 for s in range(NS)}
    for step in plan():
        if step[0] == "chunk":
            _, s, c = step
            hop(s, c).wait_recv()
            for kid, _ in KIDS.get((s, c), ()):
                hop(kid, c).start()
            parts[s] += 1
            if parts[s] == NC:
                if s < RING:
                    across(s).start()
                    col_side(s, 0)
                else:
                    row_side(s)
        elif step[0] == "half":
            s, a = step[1]
            meet(a)
            f = flip(s if s else 4)
            score[0, :, pl.ds(0, ROWS)] = lax.dot_general(
                buf[0, s, pl.ds(HEAD, ROWS), :], buf[f, a, pl.ds(HEAD, ROWS), :], (((1,), (1,)), ((), ())),
                preferred_element_type=jnp.float32,
            )
            fold(score.at[0], row_slot(s), a, halves=(f,))
        else:
            tasks = step[1]
            for _, a in tasks:
                meet(a)
            if len(tasks) == 1:
                score[0] = dot(*tasks[0])
                fold(score.at[0], row_slot(tasks[0][0]), tasks[0][1])
                continue
            n = len(tasks)
            row_at, col_at = [t[0] for t in tasks], [t[1] for t in tasks]
            score[0] = dot(*tasks[0])

            def pair(j, carry, row_at=row_at, col_at=col_at, n=n):
                def task(i):
                    return pick(row_at, i), pick(col_at, i)

                def slot_of(s):
                    return jnp.where(s == 0, 0, s - RING + 1)

                first, second = task(2 * j), task(2 * j + 1)
                score[1] = dot(*second)
                fold(score.at[0], slot_of(first[0]), first[1])
                if n > 2:
                    score[0] = dot(*task(2 * j + 2))
                fold(score.at[1], slot_of(second[0]), second[1])
                return carry

            lax.fori_loop(0, n // 2, pair, 0)

    def row_result(k):
        m = row_best[k]
        return jnp.concatenate(
            [jnp.max(m[128 * h : 128 * h + 128].T, axis=0, keepdims=True) for h in (0, 1)], axis=1
        )

    def col_result(a, h):
        return jnp.max(col_best[a, h], axis=0, keepdims=True)

    def home(n):
        s, f = HOME[n]
        return pltpu.make_async_remote_copy(
            src_ref=send_back.at[n], dst_ref=got_back.at[n], send_sem=home_out.at[n], recv_sem=home_in.at[n],
            device_id=device(SLOTS[s], f), device_id_type=MESH,
        )

    for n, (s, f) in enumerate(HOME):
        send_back[n] = row_result(row_slot(s)) if s >= RING else col_result(s, f)
        home(n).start()
    best = jnp.maximum(row_result(0), col_result(0, 0))
    for n in range(len(HOME)):
        home(n).wait_recv()
        best = jnp.maximum(best, got_back[n])
    out_ref[...] = best
    for s, c in EDGE:
        hop(s, c).wait_send()
    for a in range(RING):
        across(a).wait_send()
    for n in range(len(HOME)):
        home(n).wait_send()


def body(embeddings, cluster, order):
    f32, nr, nh = jnp.float32, NS - RING + 1, len(HOME)
    dma = pltpu.SemaphoreType.DMA
    out = pl.pallas_call(
        kernel,
        out_shape=jax.ShapeDtypeStruct((1, ROWS), f32),
        in_specs=[pl.BlockSpec(memory_space=pltpu.VMEM)] * 3,
        out_specs=pl.BlockSpec(memory_space=pltpu.VMEM),
        scratch_shapes=[
            pltpu.VMEM((2, NS, TALL, WIDTH), jnp.bfloat16),
            pltpu.VMEM((nr, ROWS, 128), f32), pltpu.VMEM((nr, ROWS, 128), f32),
            pltpu.VMEM((RING, 2, 8, ROWS), f32), pltpu.VMEM((RING, 2, 8, ROWS), f32),
            pltpu.VMEM((nr, ROWS, 128), f32), pltpu.VMEM((RING, 2, 8, ROWS), f32),
            pltpu.VMEM((2, ROWS, 2 * ROWS), f32),
            pltpu.VMEM((nh, 1, ROWS), f32), pltpu.VMEM((nh, 1, ROWS), f32),
            dma((NS, NC)), dma((NS, NC)), dma((RING,)), dma((RING,)), dma((nh,)), dma((nh,)),
        ],
        compiler_params=pltpu.CompilerParams(collective_id=0, has_side_effects=True, vmem_limit_bytes=40 * 2**20),
        cost_estimate=pl.CostEstimate(flops=10**10, bytes_accessed=2**20, transcendentals=0),
        name="nearest",
    )(embeddings, cluster.reshape(1, ROWS), order.reshape(1, ROWS))
    return out.reshape(ROWS)


def solution(mesh):
    return jax.shard_map(
        body,
        mesh=mesh,
        in_specs=(P(("grp", "blk"), None), P(("grp", "blk")), P(("grp", "blk"))),
        out_specs=P(("grp", "blk")),
        check_vma=False,
    )
```

time: 462 us -> 61.2 us (0.13)
  waiting for transfers between devices: 270 us -> 0 us
  local copies, waits for them, and re-layouts: 110 us -> 2.21 us
  Pallas kernels: 0 us -> 58.9 us
  starting transfers between devices: 33.1 us -> 0 us
  blocking collectives: 25.2 us -> 0 us
  matrix products: 16.7 us -> 0 us
    ppermute x45 -> x0, waiting for transfers between devices: 258 us -> none  [from_behind(): return lax.ppermute(x, axis, [(i, (i + by) % size) for i in range(size)])]
    scatter x3 -> x0, local copies, waits for them, and re-layouts: 103 us -> none  [the longest x1 35.4 us: body(): jnp.zeros((groups, capacity), jnp.int32).at[target, slot].set(order)]
    pallas_call x0 -> x1, Pallas kernels: none -> 58.9 us  [body(): pl.pallas_call(kernel, out_shape=jax.ShapeDtypeStruct((1, ROWS), f32), in...]
    all_to_all x1 -> x0, blocking collectives: 25.2 us -> none  [body(): lax.all_to_all(best.reshape(groups, capacity), 'grp', split_axis=0, conca...]
    all_to_all x3 -> x0, starting transfers between devices: 22.9 us -> none  [the longest x1 8.37 us: body(): lax.all_to_all(send_ord, 'grp', split_axis=0, concat_axis=0, tiled=True)]
    dot_general x16 -> x0, matrix products: 16.7 us -> none  [fold_block(): lax.dot_general(local_unit, block_unit, (((1,), (1,)), ((), ())), preferr...]
    all_to_all x3 -> x0, waiting for transfers between devices: 12 us -> none  [the longest x1 12 us: body(): lax.all_to_all(send_unit, 'grp', split_axis=0, concat_axis=0, tiled=True)]
    ppermute x45 -> x0, starting transfers between devices: 10.2 us -> none  [from_behind(): return lax.ppermute(x, axis, [(i, (i + by) % size) for i in range(size)])]
  transfers between devices with their start and end apart: 48 -> 0, of which waited for: 16 -> 0; matrix products, arithmetic and copies ran while one was open for 16% -> 0% of each run, Pallas kernels for 0% -> 0%
where the time goes in v1:
time: 61.2 us; the launch traced here: 61.1 us
  Pallas kernels  58.9 us (96%)
  local copies, waits for them, and re-layouts  2.21 us (4%)
    pallas_call x1, Pallas kernels, body(): pl.pallas_call(kernel, out_shape=jax.ShapeDtypeStruct((1, ROWS), f32), in...  58.9 us
    unnamed x7, local copies, waits for them, and re-layouts  2.21 us

profile of v1, /device:TPU:1, one launch (start us, length us, event | category | flops | bytes accessed | tf_op | source)
XLA Modules:
  0.0 61.1 jit_solution(16358486882764815983)
XLA Ops:
  0.0 0.0 copy-start.2
  0.0 0.0 copy-start.1
  0.0 0.7 %copy-done.2 = s32[256]{0:T(256)S(1)} copy-done((s32[256]{0:T(256)S(1)}, s32[256]{0:T(256)}, u32[]{:S(2)}) %copy-start.2) | copy-done | bytes 1048
  0.7 0.0 copy-done.1
  0.7 0.0 copy-start
  0.7 0.9 %copy-done = bf16[256,512]{1,0:T(8,128)(2,1)S(1)} copy-done((bf16[256,512]{1,0:T(8,128)(2,1)S(1)}, bf16[256,512]{1,0:T(8,128)(2,1)}, u32[]{:S(2)}) %copy-start) | copy-done | bytes 262168
  1.6 58.9 %nearest.1 = f32[1,256]{1,0:T(1,128)S(1)} custom-call(bf16[256,512]{1,0:T(8,128)(2,1)S(1)} %copy-done, s32[1,256]{1,0:T(1,128)S(1)} %bitcast.4, s32[1,256]{1,0:T(1,128)S(1)} %bitcast.5), custom_call_target="tpu_custom_call" | custom-call | flops 10000000000 | bytes 1048576 | tf_op jit(solution)/shard_map/nearest/pallas_call | solution.py:342
  60.5 0.6 copy.5
Async XLA Ops:
  0.0 0.7 %copy-start.2 = (s32[256]{0:T(256)S(1)}, s32[256]{0:T(256)}, u32[]{:S(2)}) copy-start(s32[256]{0:T(256)} %param.5) | copy-start | bytes 3076
  0.0 0.7 %copy-start.1 = (s32[256]{0:T(256)S(1)}, s32[256]{0:T(256)}, u32[]{:S(2)}) copy-start(s32[256]{0:T(256)} %param.4) | copy-start | bytes 3076
  0.7 0.9 %copy-start = (bf16[256,512]{1,0:T(8,128)(2,1)S(1)}, bf16[256,512]{1,0:T(8,128)(2,1)}, u32[]{:S(2)}) copy-start(bf16[256,512]{1,0:T(8,128)(2,1)} %x_ref.1) | copy-start | bytes 786436

commit v2 on v0

v2 whole, which is shorter than its diff:
```python
import jax
import jax.numpy as jnp
from jax import lax
from jax.experimental import pallas as pl
from jax.experimental.pallas import tpu as pltpu
from jax.sharding import PartitionSpec as P

MESH = pl.DeviceIdType.MESH
ROWS, WIDTH = 256, 512
HEAD = (16, 128)
CHUNKS = ((0, 64), (64, 64), (128, 64), (192, 64))
RING = 8
SLOTS = [(0, 0, z) for z in range(8)] + [
    (1, 0, 0), (0, 1, 0), (1, 1, 0), (1, 3, 0), (2, 0, 0), (0, 2, 0), (2, 1, 0), (3, 2, 0), (2, 2, 0),
]
NR = len(SLOTS) - RING + 1
SLOTS += [(3, 0, 0), (0, 3, 0)]
STEP = {"+x": (1, 0, 0), "-x": (3, 0, 0), "+y": (0, 1, 0), "-y": (0, 3, 0), "+z": (0, 0, 1), "-z": (0, 0, 7)}
FROM = {
    (0, 0, 1): ("+z", "+z"), (0, 0, 2): ("+z", "+z"), (0, 0, 3): ("+z", "+z"),
    (0, 0, 7): ("-z", "-z"), (0, 0, 6): ("-z", "-z"), (0, 0, 5): ("-z", "-z"), (0, 0, 4): ("+z", "-z"),
    (1, 0, 0): ("+x", "+x"), (3, 0, 0): ("-x", "-x"), (0, 1, 0): ("+y", "+y"), (0, 3, 0): ("-y", "-y"),
    (2, 0, 0): ("+x", "-x"), (0, 2, 0): ("+y", "-y"), (1, 1, 0): ("+x", "+y"), (1, 3, 0): ("-y", "-y"),
    (2, 1, 0): ("+x", "+y"), (3, 2, 0): ("-x", "-x"), (2, 2, 0): ("-x", "+y"),
}
NS = len(SLOTS)
NC = len(CHUNKS)
WRAP = (4, 4, 8)


def plus(a, b):
    return tuple((p + q) % w for p, q, w in zip(a, b, WRAP))


def minus(a):
    return tuple((-p) % w for p, w in zip(a, WRAP))


EDGE = {}
for s_ in range(1, NS):
    for c_ in range(NC):
        u_ = FROM[SLOTS[s_]][c_ % 2]
        EDGE[s_, c_] = (SLOTS.index(plus(SLOTS[s_], minus(STEP[u_]))), u_)
KIDS = {}
for (s_, c_), (p_, u_) in EDGE.items():
    KIDS.setdefault((p_, c_), []).append(s_)


def depth(s, c):
    return 0 if s == 0 else 1 + depth(EDGE[s, c][0], c)


def height(s, c):
    return max([0] + [1 + height(k, c) for k in KIDS.get((s, c), ())])


def arrivals(block=5.3, hop=2.0):
    at = {(0, c): 0.0 for c in range(NC)}
    free = {u: 0.0 for u in STEP}
    left = set(EDGE)
    while left:
        ready = [
            (max(at[EDGE[k][0], k[1]], free[EDGE[k][1]]), at[EDGE[k][0], k[1]], k[1], -height(*k), k[0])
            for k in left if (EDGE[k][0], k[1]) in at
        ]
        t, _, c, _, s = min(ready)
        free[EDGE[s, c][1]] = t + block / NC
        at[s, c] = t + block / NC + hop
        left.remove((s, c))
    return at


HALF_TURN = [s for s in range(RING, RING + NR - 1) if plus(SLOTS[s], SLOTS[s]) == (0, 0, 0)]
HOME = [(s, 0) for s in range(RING, RING + NR - 1)] + [(a, f) for a in range(1, RING) for f in (0, 1)] + [(0, 1)]
ITEM = 0.47


def slot_of(k):
    return 0 if k == 0 else k + RING - 1


def items(whole):
    out = []
    for a in range(RING):
        ks = [k for k in range(NR) if not (k == 0 and a in (0, 5, 6, 7)) and not (slot_of(k) in HALF_TURN and a > 4)]
        ks.sort(key=lambda k: whole[slot_of(k)])
        if len(ks) % 2:
            ks.append(ks[-1])
        for i in range(0, len(ks), 2):
            at = max(whole[slot_of(ks[i])], whole[slot_of(ks[i + 1])], whole[a] + 1.7)
            out.append((at, ks[i], ks[i + 1], a))
    return sorted(out)


def plan():
    at = arrivals()
    seen = sorted((t, c, s) for (s, c), t in at.items() if s)
    whole = {s: max(at[s, c] for c in range(NC)) for s in range(NS)}
    todo = items(whole)
    steps, now, pending, home_left = [], 0.7, None, list(range(len(HOME)))

    def homes():
        left = [i[1:] for i in todo] + ([pending] if pending else [])
        for n in list(home_left):
            s = HOME[n][0]
            if any(s == i[2] or s in (slot_of(i[0]), slot_of(i[1])) for i in left):
                continue
            steps.append(("home", n))
            home_left.remove(n)

    while todo:
        while seen and seen[0][0] <= now:
            _, c, s = seen.pop(0)
            steps.append(("chunk", s, c))
        able = [i for i in todo if i[0] <= now]
        if able and pending is None:
            steps.append(("first", able[0][1:]))
            pending = able[0][1:]
            todo.remove(able[0])
            now += ITEM / 2
            continue
        if seen:
            able = able[:2]
        able = able[: len(able) // 2 * 2]
        if len(todo) == 1 and not able and todo[0][0] <= now:
            able = todo[:1]
        if able:
            steps.append(("items", [pending] + [i[1:] for i in able]))
            pending = able[-1][1:]
            todo = [i for i in todo if i not in able]
            now += ITEM * len(able)
            if not len(able) % 2:
                homes()
        elif pending is not None and (not seen or seen[0][0] > now + 0.5):
            steps.append(("last", pending))
            pending = None
            now += ITEM / 2
        elif seen:
            now = max(now, seen[0][0])
        else:
            now += 0.1
    assert not seen
    if pending is not None:
        steps.append(("last", pending))
        pending = None
    homes()
    assert not home_left
    return steps


def pick(table, i):
    value = jnp.int32(table[-1])
    for k in range(len(table) - 2, -1, -1):
        if table[k] != table[-1]:
            value = jnp.where(i == k, jnp.int32(table[k]), value)
    return value


def kernel(x_hbm, cl_hbm, ord_hbm, out_ref, x_ref, cl_ref, ord_ref, buf, head, row_cl, row_ord, col_cl, col_ord, row_best,
           col_best, score_a, score_b, send_back, got_back, own_in, link_out, link_in, head_out, head_in, pair_out, pair_in,
           pair_head_out, pair_head_in, home_out, home_in):
    g, b = lax.axis_index("grp"), lax.axis_index("blk")
    core = g % 2
    here = (g // 4, ((g // 2) % 2) * 2 + b // 8, b % 8)
    f32, bf16 = jnp.float32, jnp.bfloat16

    loads = [
        pltpu.make_async_copy(a, v, own_in.at[n])
        for n, (a, v) in enumerate(((x_hbm, x_ref), (cl_hbm, cl_ref), (ord_hbm, ord_ref)))
    ]
    for load in loads:
        load.start()

    def device(d, flip=0):
        x, y, z = ((h + k) % w for h, k, w in zip(here, d, WRAP))
        return ((x * 2 + y // 2) * 2 + (1 - core if flip else core), (y % 2) * 8 + z)

    goes = {(minus(STEP[u]), 0) for u in STEP} | {((0, 0, 0), 1)} | {(SLOTS[s], f) for s, f in HOME}
    comes = {(minus(d), f) for d, f in goes}
    barrier = pltpu.get_barrier_semaphore()
    for d, f in sorted(comes):
        pl.semaphore_signal(barrier, inc=1, device_id=device(d, f), device_id_type=MESH)

    row_best[...] = jnp.full(row_best.shape, -1.0, f32)
    col_best[...] = jnp.full(col_best.shape, -1.0, f32)
    for load in loads:
        load.wait()
    values = x_ref[...].astype(f32)
    scale = lax.rsqrt(jnp.sum(values * values, axis=1, keepdims=True) + 1e-06)
    buf[0, 0] = (values * scale).astype(bf16)
    line = lax.broadcasted_iota(jnp.int32, HEAD, 0)
    facts = jnp.zeros(HEAD, jnp.int32)
    for h in (0, 1):
        cl, rank = cl_ref[:, pl.ds(128 * h, 128)], ord_ref[:, pl.ds(128 * h, 128)]
        for n, row in ((0, cl), (2, rank // 256), (4, rank % 256)):
            facts = jnp.where(line == n + h, row, facts)
    head[0, 0] = facts.astype(f32).astype(bf16)

    pl.semaphore_wait(barrier, len(goes))

    def hop(s, c):
        lo, n = CHUNKS[c]
        p, u = EDGE[s, c]
        return pltpu.make_async_remote_copy(
            src_ref=buf.at[0, p, pl.ds(lo, n)], dst_ref=buf.at[0, s, pl.ds(lo, n)],
            send_sem=link_out.at[s, c], recv_sem=link_in.at[s, c],
            device_id=device(minus(STEP[u])), device_id_type=MESH,
        )

    def head_hop(s):
        p, u = EDGE[s, 0]
        return pltpu.make_async_remote_copy(
            src_ref=head.at[0, p], dst_ref=head.at[0, s], send_sem=head_out.at[s], recv_sem=head_in.at[s],
            device_id=device(minus(STEP[u])), device_id_type=MESH,
        )

    def across(a):
        return [
            pltpu.make_async_remote_copy(
                src_ref=ref.at[0, a], dst_ref=ref.at[1, a], send_sem=out.at[a], recv_sem=into.at[a],
                device_id=device((0, 0, 0), 1), device_id_type=MESH,
            )
            for ref, out, into in ((buf, pair_out, pair_in), (head, pair_head_out, pair_head_in))
        ]

    def send_on(s, c):
        for kid in sorted(KIDS.get((s, c), ()), key=lambda k: -height(k, c)):
            if c == 0:
                head_hop(kid).start()
            hop(kid, c).start()

    for c in range(NC):
        send_on(0, c)
    for copy in across(0):
        copy.start()

    lines = lax.broadcasted_iota(jnp.int32, (HEAD[0], 256), 0)
    lanes = lax.broadcasted_iota(jnp.int32, (HEAD[0], 256), 1)

    def spread(h):
        low = jnp.where(lines == h, 1.0, 0.0)
        high = jnp.where(lines == 2 + h, 256.0, jnp.where(lines == 4 + h, 1.0, 0.0))
        return jnp.where(lanes < 128, low, high).astype(bf16)

    def row_side(s):
        k = 0 if s == 0 else s - RING + 1
        for h in (0, 1):
            wide = lax.dot_general(head[0, s], spread(h), (((0,), (0,)), ((), ())), preferred_element_type=f32)
            row_cl[k, pl.ds(128 * h, 128), :] = wide[:, :128]
            row_ord[k, pl.ds(128 * h, 128), :] = wide[:, 128:]

    def col_side(a, half):
        top = head[half, a].astype(f32)
        for h in (0, 1):
            at = pl.ds(128 * h, 128)
            col_cl[a, half, :, at] = jnp.broadcast_to(top[h : h + 1], (8, 128))
            col_ord[a, half, :, at] = jnp.broadcast_to(top[2 + h : 3 + h] * 256.0 + top[4 + h : 5 + h], (8, 128))

    def slot(k):
        return slot_of(k) if isinstance(k, int) else jnp.where(k == 0, 0, k + RING - 1)

    def dot(item):
        *ks, a = item
        rows = jnp.concatenate([buf[0, slot(k)] for k in ks], axis=0)
        columns = jnp.concatenate([buf[0, a], buf[1, a]], axis=0)
        return lax.dot_general(rows, columns, (((1,), (1,)), ((), ())), preferred_element_type=f32)

    tiles = [(h, t) for h in (0, 1) for t in (0, 128)]

    def fold(ref, item, both=True):
        *ks, a = item
        cl = [col_cl[a, h, :, pl.ds(t, 128)] for h, t in tiles]
        rk = [col_ord[a, h, :, pl.ds(t, 128)] for h, t in tiles]
        top = [col_best[a, h, :, pl.ds(t, 128)] for h, t in tiles] if both else None
        for m, k in enumerate(ks):
            for i in range(ROWS // 8):
                at = pl.ds(8 * i, 8)
                mine, rank, best = row_cl[k, at, :], row_ord[k, at, :], row_best[k, at, :]
                for n in range(len(tiles)):
                    s = ref[pl.ds(ROWS * m + 8 * i, 8), pl.ds(128 * n, 128)]
                    same = jnp.where(mine == cl[n], s, -1.0)
                    later = rk[n] < rank
                    best = jnp.maximum(best, jnp.where(later, same, -1.0))
                    if both:
                        top[n] = jnp.maximum(top[n], jnp.where(later, -1.0, same))
                row_best[k, at, :] = best
        if both:
            for n, (h, t) in enumerate(tiles):
                col_best[a, h, :, pl.ds(t, 128)] = top[n]

    met = set()

    def meet(a):
        if a not in met:
            met.add(a)
            for copy in across(a):
                copy.wait_recv()
            col_side(a, 1)

    def row_result(k):
        m = row_best[k]
        return jnp.concatenate(
            [jnp.max(m[128 * h : 128 * h + 128].T, axis=0, keepdims=True) for h in (0, 1)], axis=1
        )

    def col_result(a, h):
        return jnp.max(col_best[a, h], axis=0, keepdims=True)

    def home(n):
        s, f = HOME[n]
        return pltpu.make_async_remote_copy(
            src_ref=send_back.at[n], dst_ref=got_back.at[n], send_sem=home_out.at[n], recv_sem=home_in.at[n],
            device_id=device(SLOTS[s], f), device_id_type=MESH,
        )

    row_side(0)
    col_side(0, 0)
    meet(0)
    score_a[pl.ds(0, ROWS), :] = dot((0, 0))
    fold(score_a, (0, 0), both=False)

    parts = {s: 0 for s in range(NS)}
    for step in plan():
        if step[0] == "chunk":
            _, s, c = step
            hop(s, c).wait_recv()
            if c == 0:
                head_hop(s).wait_recv()
            send_on(s, c)
            parts[s] += 1
            if parts[s] == NC:
                if s < RING:
                    for copy in across(s):
                        copy.start()
                    col_side(s, 0)
                elif s < RING + NR - 1:
                    row_side(s)
        elif step[0] == "home":
            n = step[1]
            s, f = HOME[n]
            send_back[n] = row_result(s - RING + 1) if s >= RING else col_result(s, f)
            home(n).start()
        elif step[0] == "first":
            meet(step[1][2])
            score_a[...] = dot(step[1])
        elif step[0] == "last":
            fold(score_a, step[1])
        else:
            table = step[1]
            for i in table[1:]:
                meet(i[2])
            n = len(table) - 1
            if n == 1:
                score_b[...] = dot(table[1])
                fold(score_a, table[0])
                score_a[...] = score_b[...]
                continue

            def pair(j, item):
                score_b[...] = dot(item(2 * j + 1))
                fold(score_a, item(2 * j))
                score_a[...] = dot(item(2 * j + 2))
                fold(score_b, item(2 * j + 1))

            if n == 2:
                pair(0, lambda i, table=table: table[i])
            else:
                def turn(j, carry, table=table, pair=pair):
                    pair(j, lambda i: tuple(pick([t[m] for t in table], i) for m in range(3)))
                    return carry

                lax.fori_loop(0, n // 2, turn, 0)

    best = jnp.maximum(row_result(0), col_result(0, 0))
    for n in range(len(HOME)):
        home(n).wait_recv()
        best = jnp.maximum(best, got_back[n])
    out_ref[...] = best
    for s, c in EDGE:
        hop(s, c).wait_send()
        if c == 0:
            head_hop(s).wait_send()
    for a in range(RING):
        for copy in across(a):
            copy.wait_send()
    for n in range(len(HOME)):
        home(n).wait_send()


def body(embeddings, cluster, order):
    f32, bf16, i32, nh = jnp.float32, jnp.bfloat16, jnp.int32, len(HOME)
    dma = pltpu.SemaphoreType.DMA
    out = pl.pallas_call(
        kernel,
        out_shape=jax.ShapeDtypeStruct((1, ROWS), f32),
        in_specs=[pl.BlockSpec(memory_space=pl.ANY)] * 3,
        out_specs=pl.BlockSpec(memory_space=pltpu.VMEM),
        scratch_shapes=[
            pltpu.VMEM((ROWS, WIDTH), bf16), pltpu.VMEM((1, ROWS), i32), pltpu.VMEM((1, ROWS), i32),
            pltpu.VMEM((2, NS, ROWS, WIDTH), bf16), pltpu.VMEM((2, NS, *HEAD), bf16),
            pltpu.VMEM((NR, ROWS, 128), f32), pltpu.VMEM((NR, ROWS, 128), f32),
            pltpu.VMEM((RING, 2, 8, ROWS), f32), pltpu.VMEM((RING, 2, 8, ROWS), f32),
            pltpu.VMEM((NR, ROWS, 128), f32), pltpu.VMEM((RING, 2, 8, ROWS), f32),
            pltpu.VMEM((2 * ROWS, 2 * ROWS), f32), pltpu.VMEM((2 * ROWS, 2 * ROWS), f32),
            pltpu.VMEM((nh, 1, ROWS), f32), pltpu.VMEM((nh, 1, ROWS), f32), dma((3,)),
            dma((NS, NC)), dma((NS, NC)), dma((NS,)), dma((NS,)), dma((RING,)), dma((RING,)), dma((RING,)), dma((RING,)),
            dma((nh,)), dma((nh,)),
        ],
        compiler_params=pltpu.CompilerParams(collective_id=0, has_side_effects=True, vmem_limit_bytes=40 * 2**20),
        cost_estimate=pl.CostEstimate(flops=10**10, bytes_accessed=2**20, transcendentals=0),
        name="nearest",
    )(embeddings, cluster.reshape(1, ROWS), order.reshape(1, ROWS))
    return out.reshape(ROWS)


def solution(mesh):
    return jax.shard_map(
        body,
        mesh=mesh,
        in_specs=(P(("grp", "blk"), None), P(("grp", "blk")), P(("grp", "blk"))),
        out_specs=P(("grp", "blk")),
        check_vma=False,
    )
```

time: 462 us -> 54.4 us (0.12)
  waiting for transfers between devices: 270 us -> 0 us
  local copies, waits for them, and re-layouts: 110 us -> 2.21 us
  Pallas kernels: 0 us -> 52 us
  starting transfers between devices: 33.1 us -> 0 us
  blocking collectives: 25.2 us -> 0 us
  matrix products: 16.7 us -> 0 us
    ppermute x45 -> x0, waiting for transfers between devices: 258 us -> none  [from_behind(): return lax.ppermute(x, axis, [(i, (i + by) % size) for i in range(size)])]
    scatter x3 -> x0, local copies, waits for them, and re-layouts: 103 us -> none  [the longest x1 35.4 us: body(): jnp.zeros((groups, capacity), jnp.int32).at[target, slot].set(order)]
    pallas_call x0 -> x1, Pallas kernels: none -> 52 us  [body(): pl.pallas_call(kernel, out_shape=jax.ShapeDtypeStruct((1, ROWS), f32), in...]
    all_to_all x1 -> x0, blocking collectives: 25.2 us -> none  [body(): lax.all_to_all(best.reshape(groups, capacity), 'grp', split_axis=0, conca...]
    all_to_all x3 -> x0, starting transfers between devices: 22.9 us -> none  [the longest x1 8.37 us: body(): lax.all_to_all(send_ord, 'grp', split_axis=0, concat_axis=0, tiled=True)]
    dot_general x16 -> x0, matrix products: 16.7 us -> none  [fold_block(): lax.dot_general(local_unit, block_unit, (((1,), (1,)), ((), ())), preferr...]
    all_to_all x3 -> x0, waiting for transfers between devices: 12 us -> none  [the longest x1 12 us: body(): lax.all_to_all(send_unit, 'grp', split_axis=0, concat_axis=0, tiled=True)]
    ppermute x45 -> x0, starting transfers between devices: 10.2 us -> none  [from_behind(): return lax.ppermute(x, axis, [(i, (i + by) % size) for i in range(size)])]
  transfers between devices with their start and end apart: 48 -> 0, of which waited for: 16 -> 0; matrix products, arithmetic and copies ran while one was open for 16% -> 0% of each run, Pallas kernels for 0% -> 0%
where the time goes in v2:
time: 54.4 us; the launch traced here: 54.3 us
  Pallas kernels  52 us (96%)
  local copies, waits for them, and re-layouts  2.21 us (4%)
    pallas_call x1, Pallas kernels, body(): pl.pallas_call(kernel, out_shape=jax.ShapeDtypeStruct((1, ROWS), f32), in...  52 us
    unnamed x7, local copies, waits for them, and re-layouts  2.21 us

profile of v2, /device:TPU:1, one launch (start us, length us, event | category | flops | bytes accessed | tf_op | source)
XLA Modules:
  0.0 54.3 jit_solution(7415619763037769615)
XLA Ops:
  0.0 0.0 copy-start.2
  0.0 0.0 copy-start.1
  0.0 0.7 %copy-done.2 = s32[256]{0:T(256)S(1)} copy-done((s32[256]{0:T(256)S(1)}, s32[256]{0:T(256)}, u32[]{:S(2)}) %copy-start.2) | copy-done | bytes 1048
  0.7 0.0 copy-done.1
  0.7 0.0 copy-start
  0.7 0.9 %copy-done = bf16[256,512]{1,0:T(8,128)(2,1)S(1)} copy-done((bf16[256,512]{1,0:T(8,128)(2,1)S(1)}, bf16[256,512]{1,0:T(8,128)(2,1)}, u32[]{:S(2)}) %copy-start) | copy-done | bytes 262168
  1.6 52.0 %nearest.1 = f32[1,256]{1,0:T(1,128)S(1)} custom-call(bf16[256,512]{1,0:T(8,128)(2,1)S(1)} %copy-done, s32[1,256]{1,0:T(1,128)S(1)} %bitcast.4, s32[1,256]{1,0:T(1,128)S(1)} %bitcast.5), custom_call_target="tpu_custom_call" | custom-call | flops 10000000000 | bytes 1048576 | tf_op jit(solution)/shard_map/nearest/pallas_call | solution.py:393
  53.7 0.6 %copy.5 = f32[256]{0:T(256)} copy(f32[256]{0:T(256)S(1)} %bitcast.3) | data formatting | bytes 2048
Async XLA Ops:
  0.0 0.7 %copy-start.2 = (s32[256]{0:T(256)S(1)}, s32[256]{0:T(256)}, u32[]{:S(2)}) copy-start(s32[256]{0:T(256)} %param.5) | copy-start | bytes 3076
  0.0 0.7 %copy-start.1 = (s32[256]{0:T(256)S(1)}, s32[256]{0:T(256)}, u32[]{:S(2)}) copy-start(s32[256]{0:T(256)} %param.4) | copy-start | bytes 3076
  0.7 0.9 %copy-start = (bf16[256,512]{1,0:T(8,128)(2,1)S(1)}, bf16[256,512]{1,0:T(8,128)(2,1)}, u32[]{:S(2)}) copy-start(bf16[256,512]{1,0:T(8,128)(2,1)} %x_hbm.1) | copy-start | bytes 786436

commit v3 on v2

--- a/solution.py
+++ b/solution.py
@@ -72,22 +72,31 @@
 
 HALF_TURN = [s for s in range(RING, RING + NR - 1) if plus(SLOTS[s], SLOTS[s]) == (0, 0, 0)]
 HOME = [(s, 0) for s in range(RING, RING + NR - 1)] + [(a, f) for a in range(1, RING) for f in (0, 1)] + [(0, 1)]
-ITEM = 0.47
+ITEM = 0.45
+PAIR = 1.5
 
 
 def slot_of(k):
     return 0 if k == 0 else k + RING - 1
+
+
+def far(s):
+    return sum(min(p, w - p) for p, w in zip(SLOTS[s], WRAP))
+
+
+def reach(item):
+    return max(far(slot_of(item[1])), far(slot_of(item[2])), far(item[3]))
 
 
 def items(whole):
     out = []
     for a in range(RING):
         ks = [k for k in range(NR) if not (k == 0 and a in (0, 5, 6, 7)) and not (slot_of(k) in HALF_TURN and a > 4)]
-        ks.sort(key=lambda k: whole[slot_of(k)])
+        ks.sort(key=lambda k: (whole[slot_of(k)], k))
         if len(ks) % 2:
             ks.append(ks[-1])
         for i in range(0, len(ks), 2):
-            at = max(whole[slot_of(ks[i])], whole[slot_of(ks[i + 1])], whole[a] + 1.7)
+            at = max(whole[slot_of(ks[i])], whole[slot_of(ks[i + 1])], whole[a] + PAIR)
             out.append((at, ks[i], ks[i + 1], a))
     return sorted(out)
 
@@ -112,18 +121,16 @@
         while seen and seen[0][0] <= now:
             _, c, s = seen.pop(0)
             steps.append(("chunk", s, c))
-        able = [i for i in todo if i[0] <= now]
+        able = sorted((i for i in todo if i[0] <= now), key=lambda i: (-reach(i), i))
         if able and pending is None:
             steps.append(("first", able[0][1:]))
             pending = able[0][1:]
             todo.remove(able[0])
             now += ITEM / 2
             continue
-        if seen:
-            able = able[:2]
-        able = able[: len(able) // 2 * 2]
-        if len(todo) == 1 and not able and todo[0][0] <= now:
-            able = todo[:1]
+        able = able[:2]
+        if len(able) == 1 and len(todo) > 1:
+            able = []
         if able:
             steps.append(("items", [pending] + [i[1:] for i in able]))
             pending = able[-1][1:]
@@ -175,10 +182,9 @@
         x, y, z = ((h + k) % w for h, k, w in zip(here, d, WRAP))
         return ((x * 2 + y // 2) * 2 + (1 - core if flip else core), (y % 2) * 8 + z)
 
-    goes = {(minus(STEP[u]), 0) for u in STEP} | {((0, 0, 0), 1)} | {(SLOTS[s], f) for s, f in HOME}
-    comes = {(minus(d), f) for d, f in goes}
+    near = [(STEP[u], 0) for u in STEP] + [((0, 0, 0), 1)]
     barrier = pltpu.get_barrier_semaphore()
-    for d, f in sorted(comes):
+    for d, f in near:
         pl.semaphore_signal(barrier, inc=1, device_id=device(d, f), device_id_type=MESH)
 
     row_best[...] = jnp.full(row_best.shape, -1.0, f32)
@@ -196,7 +202,7 @@
             facts = jnp.where(line == n + h, row, facts)
     head[0, 0] = facts.astype(f32).astype(bf16)
 
-    pl.semaphore_wait(barrier, len(goes))
+    pl.semaphore_wait(barrier, len(near))
 
     def hop(s, c):
         lo, n = CHUNKS[c]
@@ -214,13 +220,17 @@
             device_id=device(minus(STEP[u])), device_id_type=MESH,
         )
 
-    def across(a):
+    def across(a, c):
+        lo, n = CHUNKS[c]
+        ways = [(buf.at[0, a, pl.ds(lo, n)], buf.at[1, a, pl.ds(lo, n)], pair_out.at[a, c], pair_in.at[a, c])]
+        if c == 0:
+            ways.append((head.at[0, a], head.at[1, a], pair_head_out.at[a], pair_head_in.at[a]))
         return [
             pltpu.make_async_remote_copy(
-                src_ref=ref.at[0, a], dst_ref=ref.at[1, a], send_sem=out.at[a], recv_sem=into.at[a],
+                src_ref=src, dst_ref=dst, send_sem=out, recv_sem=into,
                 device_id=device((0, 0, 0), 1), device_id_type=MESH,
             )
-            for ref, out, into in ((buf, pair_out, pair_in), (head, pair_head_out, pair_head_in))
+            for src, dst, out, into in ways
         ]
 
     def send_on(s, c):
@@ -231,8 +241,9 @@
 
     for c in range(NC):
         send_on(0, c)
-    for copy in across(0):
-        copy.start()
+    for c in range(NC):
+        for copy in across(0, c):
+            copy.start()
 
     lines = lax.broadcasted_iota(jnp.int32, (HEAD[0], 256), 0)
     lanes = lax.broadcasted_iota(jnp.int32, (HEAD[0], 256), 1)
@@ -293,8 +304,9 @@
     def meet(a):
         if a not in met:
             met.add(a)
-            for copy in across(a):
-                copy.wait_recv()
+            for c in range(NC):
+                for copy in across(a, c):
+                    copy.wait_recv()
             col_side(a, 1)
 
     def row_result(k):
@@ -327,11 +339,12 @@
             if c == 0:
                 head_hop(s).wait_recv()
             send_on(s, c)
+            if s < RING:
+                for copy in across(s, c):
+                    copy.start()
             parts[s] += 1
             if parts[s] == NC:
                 if s < RING:
-                    for copy in across(s):
-                        copy.start()
                     col_side(s, 0)
                 elif s < RING + NR - 1:
                     row_side(s)
@@ -372,17 +385,18 @@
                 lax.fori_loop(0, n // 2, turn, 0)
 
     best = jnp.maximum(row_result(0), col_result(0, 0))
-    for n in range(len(HOME)):
-        home(n).wait_recv()
-        best = jnp.maximum(best, got_back[n])
-    out_ref[...] = best
     for s, c in EDGE:
         hop(s, c).wait_send()
         if c == 0:
             head_hop(s).wait_send()
     for a in range(RING):
-        for copy in across(a):
-            copy.wait_send()
+        for c in range(NC):
+            for copy in across(a, c):
+                copy.wait_send()
+    for n in range(len(HOME)):
+        home(n).wait_recv()
+        best = jnp.maximum(best, got_back[n])
+    out_ref[...] = best
     for n in range(len(HOME)):
         home(n).wait_send()
 
@@ -403,10 +417,10 @@
             pltpu.VMEM((NR, ROWS, 128), f32), pltpu.VMEM((RING, 2, 8, ROWS), f32),
             pltpu.VMEM((2 * ROWS, 2 * ROWS), f32), pltpu.VMEM((2 * ROWS, 2 * ROWS), f32),
             pltpu.VMEM((nh, 1, ROWS), f32), pltpu.VMEM((nh, 1, ROWS), f32), dma((3,)),
-            dma((NS, NC)), dma((NS, NC)), dma((NS,)), dma((NS,)), dma((RING,)), dma((RING,)), dma((RING,)), dma((RING,)),
+            dma((NS, NC)), dma((NS, NC)), dma((NS,)), dma((NS,)), dma((RING, NC)), dma((RING, NC)), dma((RING,)), dma((RING,)),
             dma((nh,)), dma((nh,)),
         ],
-        compiler_params=pltpu.CompilerParams(collective_id=0, has_side_effects=True, vmem_limit_bytes=40 * 2**20),
+        compiler_params=pltpu.CompilerParams(collective_id=0, has_side_effects=True, vmem_limit_bytes=60 * 2**20),
         cost_estimate=pl.CostEstimate(flops=10**10, bytes_accessed=2**20, transcendentals=0),
         name="nearest",
     )(embeddings, cluster.reshape(1, ROWS), order.reshape(1, ROWS))

time: 54.4 us -> 49.7 us (0.914)
  Pallas kernels: 52 us -> 48.3 us
  local copies, waits for them, and re-layouts: 2.21 us -> 1.22 us
    pallas_call x1, Pallas kernels: 52 us -> 48.3 us  [body(): pl.pallas_call(kernel, out_shape=jax.ShapeDtypeStruct((1, ROWS), f32), in...]
    unnamed x7 -> x3, local copies, waits for them, and re-layouts: 2.21 us -> 1.22 us
where the time goes in v3:
time: 49.7 us; the launch traced here: 49.6 us
  Pallas kernels  48.3 us (97%)
  local copies, waits for them, and re-layouts  1.22 us (2%)
    pallas_call x1, Pallas kernels, body(): pl.pallas_call(kernel, out_shape=jax.ShapeDtypeStruct((1, ROWS), f32), in...  48.3 us
    unnamed x3, local copies, waits for them, and re-layouts  1.22 us

profile of v3, /device:TPU:1, one launch (start us, length us, event | category | flops | bytes accessed | tf_op | source)
XLA Modules:
  0.0 49.6 jit_solution(1804193317541908981)
XLA Ops:
  0.0 48.3 %nearest.1 = f32[1,256]{1,0:T(1,128)} custom-call(bf16[256,512]{1,0:T(8,128)(2,1)} %x_hbm.1, s32[1,256]{1,0:T(1,128)} %bitcast.4, s32[1,256]{1,0:T(1,128)} %bitcast.5), custom_call_target="tpu_custom_call" | custom-call | flops 10000000000 | bytes 1048576 | tf_op jit(solution)/shard_map/nearest/pallas_call | solution.py:407
  48.4 0.0 copy-start
  48.4 0.7 %copy-done = f32[1,256]{1,0:T(1,128)S(1)} copy-done((f32[1,256]{1,0:T(1,128)S(1)}, f32[1,256]{1,0:T(1,128)}, u32[]{:S(2)}) %copy-start) | copy-done | bytes 1048
  49.0 0.6 %copy.5 = f32[256]{0:T(256)} copy(f32[256]{0:T(256)S(1)} %bitcast.3) | data formatting | bytes 2048
Async XLA Ops:
  48.4 0.7 %copy-start = (f32[1,256]{1,0:T(1,128)S(1)}, f32[1,256]{1,0:T(1,128)}, u32[]{:S(2)}) copy-start(f32[1,256]{1,0:T(1,128)} %nearest.1) | copy-start | bytes 3076

commit v4 on v3

--- a/solution.py
+++ b/solution.py
@@ -8,7 +8,7 @@
 MESH = pl.DeviceIdType.MESH
 ROWS, WIDTH = 256, 512
 HEAD = (16, 128)
-CHUNKS = ((0, 64), (64, 64), (128, 64), (192, 64))
+CHUNKS = ((0, 128), (128, 128))
 RING = 8
 SLOTS = [(0, 0, z) for z in range(8)] + [
     (1, 0, 0), (0, 1, 0), (1, 1, 0), (1, 3, 0), (2, 0, 0), (0, 2, 0), (2, 1, 0), (3, 2, 0), (2, 2, 0),
@@ -73,7 +73,7 @@
 HALF_TURN = [s for s in range(RING, RING + NR - 1) if plus(SLOTS[s], SLOTS[s]) == (0, 0, 0)]
 HOME = [(s, 0) for s in range(RING, RING + NR - 1)] + [(a, f) for a in range(1, RING) for f in (0, 1)] + [(0, 1)]
 ITEM = 0.45
-PAIR = 1.5
+PAIR = 0.7
 
 
 def slot_of(k):
@@ -110,57 +110,43 @@
 
     def homes():
         left = [i[1:] for i in todo] + ([pending] if pending else [])
+        done = []
         for n in list(home_left):
             s = HOME[n][0]
             if any(s == i[2] or s in (slot_of(i[0]), slot_of(i[1])) for i in left):
                 continue
-            steps.append(("home", n))
+            done.append(n)
             home_left.remove(n)
+        if done:
+            steps.append(("home", done))
 
     while todo:
         while seen and seen[0][0] <= now:
             _, c, s = seen.pop(0)
             steps.append(("chunk", s, c))
-        able = sorted((i for i in todo if i[0] <= now), key=lambda i: (-reach(i), i))
-        if able and pending is None:
-            steps.append(("first", able[0][1:]))
+        able = sorted((i for i in todo if i[0] <= now), key=lambda i: (i[0], -reach(i), i))
+        if able:
+            steps.append(("item", pending, able[0][1:]))
+            now += ITEM if pending else ITEM / 2
             pending = able[0][1:]
             todo.remove(able[0])
-            now += ITEM / 2
-            continue
-        able = able[:2]
-        if len(able) == 1 and len(todo) > 1:
-            able = []
-        if able:
-            steps.append(("items", [pending] + [i[1:] for i in able]))
-            pending = able[-1][1:]
-            todo = [i for i in todo if i not in able]
-            now += ITEM * len(able)
-            if not len(able) % 2:
-                homes()
+            homes()
         elif pending is not None and (not seen or seen[0][0] > now + 0.5):
-            steps.append(("last", pending))
+            steps.append(("item", pending, None))
             pending = None
             now += ITEM / 2
+            homes()
         elif seen:
             now = max(now, seen[0][0])
         else:
             now += 0.1
     assert not seen
     if pending is not None:
-        steps.append(("last", pending))
+        steps.append(("item", pending, None))
         pending = None
     homes()
     assert not home_left
     return steps
-
-
-def pick(table, i):
-    value = jnp.int32(table[-1])
-    for k in range(len(table) - 2, -1, -1):
-        if table[k] != table[-1]:
-            value = jnp.where(i == k, jnp.int32(table[k]), value)
-    return value
 
 
 def kernel(x_hbm, cl_hbm, ord_hbm, out_ref, x_ref, cl_ref, ord_ref, buf, head, row_cl, row_ord, col_cl, col_ord, row_best,
@@ -268,7 +254,7 @@
             col_ord[a, half, :, at] = jnp.broadcast_to(top[2 + h : 3 + h] * 256.0 + top[4 + h : 5 + h], (8, 128))
 
     def slot(k):
-        return slot_of(k) if isinstance(k, int) else jnp.where(k == 0, 0, k + RING - 1)
+        return slot_of(k)
 
     def dot(item):
         *ks, a = item
@@ -332,6 +318,7 @@
     fold(score_a, (0, 0), both=False)
 
     parts = {s: 0 for s in range(NS)}
+    scores, at = (score_a, score_b), 0
     for step in plan():
         if step[0] == "chunk":
             _, s, c = step
@@ -349,40 +336,19 @@
                 elif s < RING + NR - 1:
                     row_side(s)
         elif step[0] == "home":
-            n = step[1]
-            s, f = HOME[n]
-            send_back[n] = row_result(s - RING + 1) if s >= RING else col_result(s, f)
-            home(n).start()
-        elif step[0] == "first":
-            meet(step[1][2])
-            score_a[...] = dot(step[1])
-        elif step[0] == "last":
-            fold(score_a, step[1])
+            for n in step[1]:
+                s, f = HOME[n]
+                send_back[n] = row_result(s - RING + 1) if s >= RING else col_result(s, f)
+            for n in step[1]:
+                home(n).start()
         else:
-            table = step[1]
-            for i in table[1:]:
-                meet(i[2])
-            n = len(table) - 1
-            if n == 1:
-                score_b[...] = dot(table[1])
-                fold(score_a, table[0])
-                score_a[...] = score_b[...]
-                continue
-
-            def pair(j, item):
-                score_b[...] = dot(item(2 * j + 1))
-                fold(score_a, item(2 * j))
-                score_a[...] = dot(item(2 * j + 2))
-                fold(score_b, item(2 * j + 1))
-
-            if n == 2:
-                pair(0, lambda i, table=table: table[i])
-            else:
-                def turn(j, carry, table=table, pair=pair):
-                    pair(j, lambda i: tuple(pick([t[m] for t in table], i) for m in range(3)))
-                    return carry
-
-                lax.fori_loop(0, n // 2, turn, 0)
+            _, old, new = step
+            if new is not None:
+                meet(new[2])
+                scores[1 - at][...] = dot(new)
+            if old is not None:
+                fold(scores[at], old)
+            at = 1 - at
 
     best = jnp.maximum(row_result(0), col_result(0, 0))
     for s, c in EDGE:

time: 49.7 us -> 49.5 us (level)
  no operation moved by 1% of the time
where the time goes in v4:
time: 49.5 us; the launch traced here: 49.4 us
  Pallas kernels  48.2 us (97%)
  local copies, waits for them, and re-layouts  1.22 us (2%)
    pallas_call x1, Pallas kernels, body(): pl.pallas_call(kernel, out_shape=jax.ShapeDtypeStruct((1, ROWS), f32), in...  48.2 us
    unnamed x3, local copies, waits for them, and re-layouts  1.22 us

profile of v4, /device:TPU:1, one launch (start us, length us, event | category | flops | bytes accessed | tf_op | source)
XLA Modules:
  0.0 49.4 jit_solution(17168538099588007096)
XLA Ops:
  0.0 48.2 %nearest.1 = f32[1,256]{1,0:T(1,128)} custom-call(bf16[256,512]{1,0:T(8,128)(2,1)} %x_hbm.1, s32[1,256]{1,0:T(1,128)} %bitcast.4, s32[1,256]{1,0:T(1,128)} %bitcast.5), custom_call_target="tpu_custom_call" | custom-call | flops 10000000000 | bytes 1048576 | tf_op jit(solution)/shard_map/nearest/pallas_call | solution.py:373
  48.2 0.0 copy-start
  48.2 0.7 %copy-done = f32[1,256]{1,0:T(1,128)S(1)} copy-done((f32[1,256]{1,0:T(1,128)S(1)}, f32[1,256]{1,0:T(1,128)}, u32[]{:S(2)}) %copy-start) | copy-done | bytes 1048
  48.8 0.6 %copy.5 = f32[256]{0:T(256)} copy(f32[256]{0:T(256)S(1)} %bitcast.3) | data formatting | bytes 2048
Async XLA Ops:
  48.2 0.7 %copy-start = (f32[1,256]{1,0:T(1,128)S(1)}, f32[1,256]{1,0:T(1,128)}, u32[]{:S(2)}) copy-start(f32[1,256]{1,0:T(1,128)} %nearest.1) | copy-start | bytes 3076

commit v5 on v4

--- a/solution.py
+++ b/solution.py
@@ -11,7 +11,7 @@
 CHUNKS = ((0, 128), (128, 128))
 RING = 8
 SLOTS = [(0, 0, z) for z in range(8)] + [
-    (1, 0, 0), (0, 1, 0), (1, 1, 0), (1, 3, 0), (2, 0, 0), (0, 2, 0), (2, 1, 0), (3, 2, 0), (2, 2, 0),
+    (1, 0, 0), (0, 1, 0), (3, 3, 0), (1, 3, 0), (2, 3, 0), (1, 2, 0), (2, 0, 0), (0, 2, 0), (2, 2, 0),
 ]
 NR = len(SLOTS) - RING + 1
 SLOTS += [(3, 0, 0), (0, 3, 0)]
@@ -20,8 +20,8 @@
     (0, 0, 1): ("+z", "+z"), (0, 0, 2): ("+z", "+z"), (0, 0, 3): ("+z", "+z"),
     (0, 0, 7): ("-z", "-z"), (0, 0, 6): ("-z", "-z"), (0, 0, 5): ("-z", "-z"), (0, 0, 4): ("+z", "-z"),
     (1, 0, 0): ("+x", "+x"), (3, 0, 0): ("-x", "-x"), (0, 1, 0): ("+y", "+y"), (0, 3, 0): ("-y", "-y"),
-    (2, 0, 0): ("+x", "-x"), (0, 2, 0): ("+y", "-y"), (1, 1, 0): ("+x", "+y"), (1, 3, 0): ("-y", "-y"),
-    (2, 1, 0): ("+x", "+y"), (3, 2, 0): ("-x", "-x"), (2, 2, 0): ("-x", "+y"),
+    (3, 3, 0): ("-x", "-y"), (1, 3, 0): ("-y", "+x"), (2, 3, 0): ("-x", "+x"), (1, 2, 0): ("+x", "-y"),
+    (2, 0, 0): ("-x", "+y"), (0, 2, 0): ("+y", "+y"), (2, 2, 0): ("-y", "+x"),
 }
 NS = len(SLOTS)
 NC = len(CHUNKS)

time: 49.5 us -> 48.9 us (0.988)
  Pallas kernels: 48.2 us -> 47.6 us
    pallas_call x1, Pallas kernels: 48.2 us -> 47.6 us  [body(): pl.pallas_call(kernel, out_shape=jax.ShapeDtypeStruct((1, ROWS), f32), in...]
where the time goes in v5:
time: 48.9 us; the launch traced here: 48.8 us
  Pallas kernels  47.6 us (97%)
  local copies, waits for them, and re-layouts  1.22 us (2%)
    pallas_call x1, Pallas kernels, body(): pl.pallas_call(kernel, out_shape=jax.ShapeDtypeStruct((1, ROWS), f32), in...  47.6 us
    unnamed x3, local copies, waits for them, and re-layouts  1.22 us

profile of v5, /device:TPU:1, one launch (start us, length us, event | category | flops | bytes accessed | tf_op | source)
XLA Modules:
  0.0 48.8 jit_solution(7292520191701916316)
XLA Ops:
  0.0 47.6 %nearest.1 = f32[1,256]{1,0:T(1,128)} custom-call(bf16[256,512]{1,0:T(8,128)(2,1)} %x_hbm.1, s32[1,256]{1,0:T(1,128)} %bitcast.4, s32[1,256]{1,0:T(1,128)} %bitcast.5), custom_call_target="tpu_custom_call" | custom-call | flops 10000000000 | bytes 1048576 | tf_op jit(solution)/shard_map/nearest/pallas_call | solution.py:373
  47.6 0.0 copy-start
  47.6 0.7 %copy-done = f32[1,256]{1,0:T(1,128)S(1)} copy-done((f32[1,256]{1,0:T(1,128)S(1)}, f32[1,256]{1,0:T(1,128)}, u32[]{:S(2)}) %copy-start) | copy-done | bytes 1048
  48.3 0.6 %copy.5 = f32[256]{0:T(256)} copy(f32[256]{0:T(256)S(1)} %bitcast.3) | data formatting | bytes 2048
Async XLA Ops:
  47.6 0.7 %copy-start = (f32[1,256]{1,0:T(1,128)S(1)}, f32[1,256]{1,0:T(1,128)}, u32[]{:S(2)}) copy-start(f32[1,256]{1,0:T(1,128)} %nearest.1) | copy-start | bytes 3076
